TPU v7x, 32 devices: a whole 2x2x4 slice. The times are simulated.
32 devices in a mesh: fsdp: 4 (over z), context: 4 (over x, core), tensor: 2 (over y).
Axes of the slice: x: 2, y: 2, z: 4, core: 2. Of those that a mesh axis runs over, the one named last changes fastest.
Arguments:
- latents: bfloat16 [8, 1024, 1408], P('fsdp', ('context', 'tensor')), may hold values from -6 to 6
- skip_inputs: bfloat16 [2, 8, 1024, 1408], P(None, 'fsdp', ('context', 'tensor')), may hold values from -6 to 6
- text_states: bfloat16 [8, 333, 1024], P('fsdp'), may hold values from -6 to 6
- condition: bfloat16 [8, 1408], P('fsdp'), may hold values from -6 to 6
- positions: int32 [8, 2, 1024], P('fsdp', None, 'context'), may hold values from 0 to 63, as said below
- cotangent: bfloat16 [8, 1024, 1408], P('fsdp', ('context', 'tensor')), may hold values from -6 to 6
- skip_weight: float32 [2, 2816, 1408], P(None, ('fsdp', 'context'), 'tensor'), may hold values from -0.109375 to 0.109375
- mod_weight: float32 [2, 1408, 8448], P(None, ('fsdp', 'context'), 'tensor'), may hold values from -0.15625 to 0.15625
- proj_weight: float32 [2, 1408, 4, 1408], P(None, ('fsdp', 'context'), None, 'tensor'), may hold values from -0.15625 to 0.15625
- output_weight: float32 [2, 2, 1408, 1408], P(None, None, 'tensor', ('fsdp', 'context')), may hold values from -0.625 to 0.625
- text_weight: float32 [2, 1024, 2, 1408], P(None, ('fsdp', 'context'), None, 'tensor'), may hold values from -0.1875 to 0.1875
- up_weight: float32 [2, 1408, 6144], P(None, ('fsdp', 'context'), 'tensor'), may hold values from -0.15625 to 0.15625
- down_weight: float32 [2, 6144, 1408], P(None, 'tensor', ('fsdp', 'context')), may hold values from -0.078125 to 0.078125
- skip_momentum: float32 [2, 2816, 1408], P(None, ('fsdp', 'context'), 'tensor'), may hold values from -160 to 160
- mod_momentum: float32 [2, 1408, 8448], P(None, ('fsdp', 'context'), 'tensor'), may hold values from -160 to 160
- proj_momentum: float32 [2, 1408, 4, 1408], P(None, ('fsdp', 'context'), None, 'tensor'), may hold values from -160 to 160
- output_momentum: float32 [2, 2, 1408, 1408], P(None, None, 'tensor', ('fsdp', 'context')), may hold values from -160 to 160
- text_momentum: float32 [2, 1024, 2, 1408], P(None, ('fsdp', 'context'), None, 'tensor'), may hold values from -160 to 160
- up_momentum: float32 [2, 1408, 6144], P(None, ('fsdp', 'context'), 'tensor'), may hold values from -160 to 160
- down_momentum: float32 [2, 6144, 1408], P(None, 'tensor', ('fsdp', 'context')), may hold values from -160 to 160
- skip_average: float32 [2, 2816, 1408], P(None, ('fsdp', 'context'), 'tensor'), may hold values from -0.109375 to 0.109375
- mod_average: float32 [2, 1408, 8448], P(None, ('fsdp', 'context'), 'tensor'), may hold values from -0.15625 to 0.15625
- proj_average: float32 [2, 1408, 4, 1408], P(None, ('fsdp', 'context'), None, 'tensor'), may hold values from -0.15625 to 0.15625
- output_average: float32 [2, 2, 1408, 1408], P(None, None, 'tensor', ('fsdp', 'context')), may hold values from -0.625 to 0.625
- text_average: float32 [2, 1024, 2, 1408], P(None, ('fsdp', 'context'), None, 'tensor'), may hold values from -0.1875 to 0.1875
- up_average: float32 [2, 1408, 6144], P(None, ('fsdp', 'context'), 'tensor'), may hold values from -0.15625 to 0.15625
- down_average: float32 [2, 6144, 1408], P(None, 'tensor', ('fsdp', 'context')), may hold values from -0.078125 to 0.078125
Outputs:
- block_output: bfloat16 [8, 1024, 1408], P('fsdp', ('context', 'tensor'))
- latents_grad: float32 [8, 1024, 1408], P('fsdp', ('context', 'tensor'))
- skips_grad: float32 [2, 8, 1024, 1408], P(None, 'fsdp', ('context', 'tensor'))
- text_grad: float32 [8, 333, 1024], P('fsdp')
- condition_grad: float32 [8, 1408], P('fsdp')
- new_skip_weight: float32 [2, 2816, 1408], P(None, ('fsdp', 'context'), 'tensor')
- new_mod_weight: float32 [2, 1408, 8448], P(None, ('fsdp', 'context'), 'tensor')
- new_proj_weight: float32 [2, 1408, 4, 1408], P(None, ('fsdp', 'context'), None, 'tensor')
- new_output_weight: float32 [2, 2, 1408, 1408], P(None, None, 'tensor', ('fsdp', 'context'))
- new_text_weight: float32 [2, 1024, 2, 1408], P(None, ('fsdp', 'context'), None, 'tensor')
- new_up_weight: float32 [2, 1408, 6144], P(None, ('fsdp', 'context'), 'tensor')
- new_down_weight: float32 [2, 6144, 1408], P(None, 'tensor', ('fsdp', 'context'))
- new_skip_momentum: float32 [2, 2816, 1408], P(None, ('fsdp', 'context'), 'tensor')
- new_mod_momentum: float32 [2, 1408, 8448], P(None, ('fsdp', 'context'), 'tensor')
- new_proj_momentum: float32 [2, 1408, 4, 1408], P(None, ('fsdp', 'context'), None, 'tensor')
- new_output_momentum: float32 [2, 2, 1408, 1408], P(None, None, 'tensor', ('fsdp', 'context'))
- new_text_momentum: float32 [2, 1024, 2, 1408], P(None, ('fsdp', 'context'), None, 'tensor')
- new_up_momentum: float32 [2, 1408, 6144], P(None, ('fsdp', 'context'), 'tensor')
- new_down_momentum: float32 [2, 6144, 1408], P(None, 'tensor', ('fsdp', 'context'))
- new_skip_average: float32 [2, 2816, 1408], P(None, ('fsdp', 'context'), 'tensor')
- new_mod_average: float32 [2, 1408, 8448], P(None, ('fsdp', 'context'), 'tensor')
- new_proj_average: float32 [2, 1408, 4, 1408], P(None, ('fsdp', 'context'), None, 'tensor')
- new_output_average: float32 [2, 2, 1408, 1408], P(None, None, 'tensor', ('fsdp', 'context'))
- new_text_average: float32 [2, 1024, 2, 1408], P(None, ('fsdp', 'context'), None, 'tensor')
- new_up_average: float32 [2, 1408, 6144], P(None, ('fsdp', 'context'), 'tensor')
- new_down_average: float32 [2, 6144, 1408], P(None, 'tensor', ('fsdp', 'context'))
Inputs may be any that keep to these rules, and one draw needn't show every extreme that they name: For each sequence, positions[s, 0, i] and positions[s, 1, i] are i // w and i % w for a grid width w that is 64, 32 or 16; at least one sequence of every draw has width 1024 // 64.
All inputs are finite; a program needn't handle non-finite values.
Results may differ from a plain program's by a relative error of at most 0.025.
Values may be sent and summed in bfloat16 or wider, within the bound.
A program may use at most 512 MiB of HBM per device.

v0:
```python
import math
from types import SimpleNamespace
import jax
import jax.numpy as jnp
from jax import lax
from jax.experimental import pallas as pl
from jax.experimental.pallas import tpu as pltpu
from jax.sharding import PartitionSpec as P

HD = 88
EPSILON = 1e-06
SCORE_SCALE = 1.0 / math.sqrt(HD)
LOW = jnp.bfloat16
MIB = 1 << 20


def vmem(mebibytes):
    return pltpu.CompilerParams(vmem_limit_bytes=mebibytes * MIB)


TOKEN = jax.ShapeDtypeStruct((8, 128), jnp.float32)
TOKEN_SPEC = pl.BlockSpec((8, 128), lambda *place: (0, 0))
FREE = pl.BlockSpec(memory_space=pl.ANY)
IN_HBM = pl.BlockSpec(memory_space=pltpu.HBM)
WHOLE = pl.BlockSpec(memory_space=pltpu.VMEM)


def cost(flops, moved, transcendentals=0):
    share = 1000
    return pl.CostEstimate(
        flops=flops // share,
        bytes_accessed=moved // share,
        transcendentals=transcendentals // share,
    )


def mark(token_ref):
    token_ref[...] = jnp.zeros(token_ref.shape, jnp.float32)


def gate(operand, after):
    return pl.pallas_call(
        lambda *refs: None,
        in_specs=[IN_HBM] + [FREE] * len(after),
        out_specs=IN_HBM,
        out_shape=jax.ShapeDtypeStruct(operand.shape, operand.dtype),
        input_output_aliases={0: 0},
    )(operand, *after)


def contract(left, right, left_dim, right_dim):
    return lax.dot_general(
        left, right, (((left_dim,), (right_dim,)), ((), ())), preferred_element_type=jnp.float32
    )


def head(operand, index):
    return operand[:, index * HD : (index + 1) * HD]


def head_marks(width):
    heads = width // HD
    column = lax.broadcasted_iota(jnp.int32, (width, heads), 0)
    first = lax.broadcasted_iota(jnp.int32, (width, heads), 1) * HD
    return jnp.where((column >= first) & (column < first + HD), 1.0, 0.0).astype(LOW)


def halves(operand):
    upper = operand.astype(LOW)
    return upper, (operand - upper.astype(jnp.float32)).astype(LOW)


def head_mean(operand, marks):
    return contract(operand.astype(LOW), marks, 1, 0) / HD


def to_columns(operand, marks):
    upper, lower = halves(operand)
    return contract(upper, marks, 1, 1) + contract(lower, marks, 1, 1)


def root_factor(operand, marks):
    return to_columns(lax.rsqrt(head_mean(operand * operand, marks) + EPSILON), marks)


def root_back(operand, upstream, marks):
    factor = root_factor(operand, marks)
    normed = operand * factor
    mean = head_mean(upstream * normed, marks).astype(LOW)
    return factor * (upstream - normed * contract(mean, marks, 1, 1))


def swap_quarters(operand):
    quarter = HD // 4
    column = lax.broadcasted_iota(jnp.int32, operand.shape, 1)
    left = jnp.concatenate([operand[:, quarter:], operand[:, :quarter]], axis=-1)
    right = jnp.concatenate([operand[:, -quarter:], operand[:, :-quarter]], axis=-1)
    return jnp.where(column % (2 * quarter) < quarter, left, right)


def turn_kernel(query_ref, key_ref, cos_ref, sin_ref, *refs):
    query_out, key_out, token_ref = refs[-3:]
    mark(token_ref)
    cos, sin = cos_ref[...], sin_ref[...]
    marks = head_marks(cos.shape[1])
    for source, target in ((query_ref, query_out), (key_ref, key_out)):
        value = source[...]
        value = value * root_factor(value, marks)
        target[...] = (value * cos + swap_quarters(value) * sin).astype(LOW)


def row_blocks(operand):
    rows, width = operand.shape
    return pl.BlockSpec((min(rows, 128), width), lambda i: (i, 0))


def turn(query_raw, key_raw, cos, sin, after):
    rows, width = query_raw.shape
    spec = row_blocks(query_raw)
    shape = jax.ShapeDtypeStruct((rows, width), LOW)
    return pl.pallas_call(
        turn_kernel,
        grid=(rows // min(rows, 128),),
        in_specs=[spec] * 4 + [FREE] * len(after),
        out_specs=[spec, spec, TOKEN_SPEC],
        out_shape=[shape, shape, TOKEN],
        compiler_params=vmem(32),
        cost_estimate=cost(100 * rows * width, 20 * rows * width),
    )(query_raw, key_raw, cos, sin, *after)


def turn_back_kernel(grad_ref, raw_ref, cos_ref, sin_ref, *refs):
    out_ref, token_ref = refs[-2:]
    mark(token_ref)
    cos, sin = cos_ref[...], sin_ref[...]
    grad = grad_ref[...].astype(jnp.float32)
    grad = grad * cos - swap_quarters(grad) * sin
    out_ref[...] = root_back(raw_ref[...], grad, head_marks(cos.shape[1])).astype(LOW)


def turn_back(grad, raw, cos, sin, after):
    rows, width = raw.shape
    spec = row_blocks(raw)
    return pl.pallas_call(
        turn_back_kernel,
        grid=(rows // min(rows, 128),),
        in_specs=[spec] * 4 + [FREE] * len(after),
        out_specs=[spec, TOKEN_SPEC],
        out_shape=[jax.ShapeDtypeStruct((rows, width), LOW), TOKEN],
        compiler_params=vmem(32),
        cost_estimate=cost(100 * rows * width, 16 * rows * width),
    )(grad, raw, cos, sin, *after)


def root_kernel(raw_ref, *refs):
    out_ref, token_ref = refs[-2:]
    mark(token_ref)
    raw = raw_ref[...]
    out_ref[...] = (raw * root_factor(raw, head_marks(raw.shape[1]))).astype(LOW)


def root(raw, after):
    rows, width = raw.shape
    spec = row_blocks(raw)
    return pl.pallas_call(
        root_kernel,
        grid=(rows // min(rows, 128),),
        in_specs=[spec] + [FREE] * len(after),
        out_specs=[spec, TOKEN_SPEC],
        out_shape=[jax.ShapeDtypeStruct((rows, width), LOW), TOKEN],
        compiler_params=vmem(32),
        cost_estimate=cost(50 * rows * width, 6 * rows * width),
    )(raw, *after)


def flat(ref):
    value = ref[...]
    return value.reshape(value.shape[0] * value.shape[2], value.shape[3])


def attend_kernel(count, query_ref, *refs):
    keys, values = refs[:count], refs[count : 2 * count]
    out_ref, lse_ref = refs[-2:]
    query = flat(query_ref)
    keys = [flat(ref) for ref in keys]
    values = [flat(ref) for ref in values]
    pieces = []
    for index in range(query.shape[1] // HD):
        query_head = head(query, index)
        scores = [contract(head(key, index), query_head, 1, 1) for key in keys]
        peak = scores[0].max(axis=0, keepdims=True)
        for score in scores[1:]:
            peak = jnp.maximum(peak, score.max(axis=0, keepdims=True))
        mass = 0.0
        out = 0.0
        for score, value in zip(scores, values):
            weight = jnp.exp((score - peak) * SCORE_SCALE)
            mass = mass + weight.sum(axis=0, keepdims=True)
            out = out + contract(head(value, index), weight.astype(LOW), 0, 0)
        pieces.append((out / mass).T.astype(LOW))
        lse_ref[0, index : index + 1, :] = peak * SCORE_SCALE + jnp.log(mass)
    out_ref[...] = jnp.concatenate(pieces, axis=-1).reshape(out_ref.shape)


def block_of(operand):
    parts, _, tokens, width = operand.shape
    return pl.BlockSpec((parts, 1, tokens, width), lambda s: (0, s, 0, 0))


def attend(query, keys, values, after):
    parts, seqs, tokens, width = query.shape
    heads = width // HD
    count = len(keys)
    pairs = seqs * heads * (parts * tokens) ** 2 * count
    return pl.pallas_call(
        lambda *refs: attend_kernel(count, *refs),
        grid=(seqs,),
        in_specs=[block_of(query)] * (1 + 2 * count) + [FREE] * len(after),
        out_specs=[
            block_of(query),
            pl.BlockSpec((1, heads, parts * tokens), lambda s: (s, 0, 0)),
        ],
        out_shape=[
            jax.ShapeDtypeStruct(query.shape, LOW),
            jax.ShapeDtypeStruct((seqs, heads, parts * tokens), jnp.float32),
        ],
        compiler_params=vmem(48),
        cost_estimate=cost(8 * pairs * 128, 20 * query.size, pairs),
    )(query, *keys, *values, *after)


def attend_back_kernel(count, query_ref, raw_ref, grad_ref, lse_ref, cos_ref, sin_ref, *refs):
    key_refs, value_refs = refs[:count], refs[count : 2 * count]
    outs = refs[-2 * count - 2 :]
    query_out, key_outs, value_outs = outs[0], outs[1 : count + 1], outs[count + 1 : -1]
    mark(outs[-1])
    query, raw, grad = flat(query_ref), flat(raw_ref), flat(grad_ref)
    cos, sin = flat(cos_ref), flat(sin_ref)
    keys = [flat(ref) for ref in key_refs]
    values = [flat(ref) for ref in value_refs]
    query_pieces = []
    key_pieces = [[] for _ in keys]
    value_pieces = [[] for _ in keys]
    for index in range(query.shape[1] // HD):
        query_head, grad_head = head(query, index), head(grad, index)
        lse = lse_ref[0, index : index + 1, :]
        weights = []
        weight_grads = []
        delta = 0.0
        for key, value in zip(keys, values):
            weight = jnp.exp(contract(head(key, index), query_head, 1, 1) * SCORE_SCALE - lse)
            weight_grad = contract(head(value, index), grad_head, 1, 1)
            delta = delta + (weight * weight_grad).sum(axis=0, keepdims=True)
            weights.append(weight)
            weight_grads.append(weight_grad)
        query_grad = 0.0
        for place, key in enumerate(keys):
            weight = weights[place]
            score_grad = (weight * (weight_grads[place] - delta)).astype(LOW)
            query_grad = query_grad + contract(head(key, index), score_grad, 0, 0)
            key_pieces[place].append(
                (contract(score_grad, query_head, 1, 0) * SCORE_SCALE).astype(LOW)
            )
            value_pieces[place].append(contract(weight.astype(LOW), grad_head, 1, 0).astype(LOW))
        query_pieces.append(query_grad.T * SCORE_SCALE)
    query_grad = jnp.concatenate(query_pieces, axis=-1)
    query_grad = query_grad * cos - swap_quarters(query_grad) * sin
    query_grad = root_back(raw, query_grad, head_marks(raw.shape[1]))
    query_out[...] = query_grad.astype(LOW).reshape(query_out.shape)
    for target, pieces in zip(key_outs, key_pieces):
        target[...] = jnp.concatenate(pieces, axis=-1).reshape(target.shape)
    for target, pieces in zip(value_outs, value_pieces):
        target[...] = jnp.concatenate(pieces, axis=-1).reshape(target.shape)


def attend_back(query, raw, grad, lse, cos, sin, keys, values, after):
    parts, seqs, tokens, width = query.shape
    heads = width // HD
    count = len(keys)
    pairs = seqs * heads * (parts * tokens) ** 2 * count
    shape = jax.ShapeDtypeStruct(query.shape, LOW)
    spec = block_of(query)
    outs = pl.pallas_call(
        lambda *refs: attend_back_kernel(count, *refs),
        grid=(seqs,),
        in_specs=[
            spec,
            spec,
            spec,
            pl.BlockSpec((1, heads, parts * tokens), lambda s: (s, 0, 0)),
            block_of(cos),
            block_of(sin),
        ]
        + [spec] * (2 * count)
        + [FREE] * len(after),
        out_specs=[spec] * (1 + 2 * count) + [TOKEN_SPEC],
        out_shape=[shape] * (1 + 2 * count) + [TOKEN],
        compiler_params=vmem(56),
        cost_estimate=cost(20 * pairs * 128, 40 * query.size, pairs),
    )(query, raw, grad, lse, cos, sin, *keys, *values, *after)
    return outs[0], list(outs[1 : 1 + count]), list(outs[1 + count : -1]), outs[-1]


def text_probs(query, key, index, count):
    scores = contract(head(key, index), head(query, index), 1, 1) * SCORE_SCALE
    inside = lax.broadcasted_iota(jnp.int32, scores.shape, 0) < count
    scores = jnp.where(inside, scores, -1e30)
    weight = jnp.exp(scores - scores.max(axis=0, keepdims=True))
    return weight / weight.sum(axis=0, keepdims=True)


def cross_kernel(count, raw_ref, key_ref, value_ref, *refs):
    out_ref, token_ref = refs[-2:]
    mark(token_ref)
    raw, key, value = raw_ref[0], key_ref[0], value_ref[0]
    query = (raw * root_factor(raw, head_marks(raw.shape[1]))).astype(LOW)
    pieces = []
    for index in range(value.shape[1] // HD):
        probs = text_probs(query, key, index, count)
        pieces.append(contract(head(value, index), probs.astype(LOW), 0, 0).T.astype(LOW))
    out_ref[0] = jnp.concatenate(pieces, axis=-1)


def sequence_block(operand):
    return pl.BlockSpec((1,) + operand.shape[1:], lambda s: (s, 0, 0))


def cross(query_raw, key, value, count, after):
    seqs, tokens, width = query_raw.shape
    pairs = seqs * tokens * key.shape[1] * (width // HD)
    return pl.pallas_call(
        lambda *refs: cross_kernel(count, *refs),
        grid=(seqs,),
        in_specs=[sequence_block(operand) for operand in (query_raw, key, value)]
        + [FREE] * len(after),
        out_specs=[sequence_block(query_raw), TOKEN_SPEC],
        out_shape=[jax.ShapeDtypeStruct(query_raw.shape, LOW), TOKEN],
        compiler_params=vmem(32),
        cost_estimate=cost(8 * pairs * 128, 6 * query_raw.size + 4 * key.size, pairs),
    )(query_raw, key, value, *after)


def cross_back_kernel(count, raw_ref, key_raw_ref, key_ref, value_ref, grad_ref, *refs):
    query_out, key_out, value_out, token_ref = refs[-4:]
    mark(token_ref)
    raw, key_raw = raw_ref[0], key_raw_ref[0]
    key, value, grad = key_ref[0], value_ref[0], grad_ref[0]
    marks = head_marks(raw.shape[1])
    query = (raw * root_factor(raw, marks)).astype(LOW)
    query_pieces, key_pieces, value_pieces = [], [], []
    for index in range(value.shape[1] // HD):
        probs = text_probs(query, key, index, count)
        grad_head = head(grad, index)
        probs_grad = contract(head(value, index), grad_head, 1, 1)
        delta = (probs * probs_grad).sum(axis=0, keepdims=True)
        score_grad = (probs * (probs_grad - delta)).astype(LOW)
        query_pieces.append(contract(head(key, index), score_grad, 0, 0).T * SCORE_SCALE)
        key_pieces.append(contract(score_grad, head(query, index), 1, 0) * SCORE_SCALE)
        value_pieces.append(contract(probs.astype(LOW), grad_head, 1, 0).astype(LOW))
    query_grad = jnp.concatenate(query_pieces, axis=-1)
    query_out[0] = root_back(raw, query_grad, marks).astype(LOW)
    key_grad = jnp.concatenate(key_pieces, axis=-1)
    key_out[0] = root_back(key_raw, key_grad, marks).astype(LOW)
    value_out[0] = jnp.concatenate(value_pieces, axis=-1)


def cross_back(query_raw, key_raw, key, value, grad, count, after):
    seqs, tokens, width = query_raw.shape
    pairs = seqs * tokens * key_raw.shape[1] * (width // HD)
    return pl.pallas_call(
        lambda *refs: cross_back_kernel(count, *refs),
        grid=(seqs,),
        in_specs=[sequence_block(operand) for operand in (query_raw, key_raw, key, value, grad)]
        + [FREE] * len(after),
        out_specs=[sequence_block(operand) for operand in (query_raw, key_raw, value)]
        + [TOKEN_SPEC],
        out_shape=[
            jax.ShapeDtypeStruct(operand.shape, LOW) for operand in (query_raw, key_raw, value)
        ]
        + [TOKEN],
        compiler_params=vmem(40),
        cost_estimate=cost(20 * pairs * 128, 10 * query_raw.size + 10 * key_raw.size, pairs),
    )(query_raw, key_raw, key, value, grad, *after)


def spread_kernel(cos_ref, sin_ref, cos_out, sin_out):
    for source, target in ((cos_ref, cos_out), (sin_ref, sin_out)):
        target[...] = jnp.concatenate([source[...]] * (target.shape[1] // HD), axis=-1)


def spread_heads(cos, sin, width):
    shape = jax.ShapeDtypeStruct((cos.shape[0], width), jnp.float32)
    return pl.pallas_call(
        spread_kernel,
        in_specs=[WHOLE] * 2,
        out_specs=[WHOLE] * 2,
        out_shape=[shape] * 2,
        compiler_params=vmem(32),
    )(cos, sin)


def add_kernel(count, cut, *refs):
    outs = refs[-count - 1 : -1]
    mark(refs[-1])
    for index in range(count):
        left, right = refs[2 * index][0], refs[2 * index + 1][0]
        total = left.astype(jnp.float32) + right.astype(jnp.float32)
        if cut:
            total = total.reshape(cut, -1, total.shape[1])
            outs[index][:, 0] = total.astype(LOW)
        else:
            outs[index][0] = total.astype(LOW)


def add_pairs(pairs, cut, after):
    count, rows, width = pairs[0][0].shape
    spec = pl.BlockSpec((1, rows, width), lambda j: (j, 0, 0))
    if cut:
        out_spec = pl.BlockSpec((cut, 1, rows // cut, width), lambda j: (0, j, 0, 0))
        shape = jax.ShapeDtypeStruct((cut, count, rows // cut, width), LOW)
    else:
        out_spec = spec
        shape = jax.ShapeDtypeStruct((count, rows, width), LOW)
    operands = [operand for pair in pairs for operand in pair]
    return pl.pallas_call(
        lambda *refs: add_kernel(len(pairs), cut, *refs),
        grid=(count,),
        in_specs=[spec] * len(operands) + [FREE] * len(after),
        out_specs=[out_spec] * len(pairs) + [TOKEN_SPEC],
        out_shape=[shape] * len(pairs) + [TOKEN],
        compiler_params=vmem(40),
        cost_estimate=cost(len(pairs) * pairs[0][0].size, 6 * len(pairs) * pairs[0][0].size),
    )(*operands, *after)


D = 1408
FF = 6144
DT = 1024
MOMENTUM = 0.9
AVERAGE_DECAY = 0.8
RATE_FACTOR = 0.5
ROPE_BASE = 10000.0
PRECISE = lax.Precision.HIGHEST
FSDP, CONTEXT, TENSOR = "fsdp", "context", "tensor"
MESH = pl.DeviceIdType.MESH


def low(operand):
    return operand.astype(LOW)


def wide(operand):
    return operand.astype(jnp.float32)


def layer_norm(operand):
    centred = operand - jnp.mean(operand, axis=-1, keepdims=True)
    return centred * lax.rsqrt(jnp.mean(centred * centred, axis=-1, keepdims=True) + EPSILON)


def layer_norm_back(operand, upstream):
    centred = operand - jnp.mean(operand, axis=-1, keepdims=True)
    factor = lax.rsqrt(jnp.mean(centred * centred, axis=-1, keepdims=True) + EPSILON)
    normed = centred * factor
    return factor * (
        upstream
        - jnp.mean(upstream, axis=-1, keepdims=True)
        - normed * jnp.mean(upstream * normed, axis=-1, keepdims=True)
    )


CORE, CHIP = 1, 2


def in_rows(operand):
    rows, width = operand.shape[-2:]
    if width % 128 and rows % 128 == 0:
        return operand.reshape(-1, 8, width)
    return operand


def swap_context(operand, bit):
    size = lax.axis_size(CONTEXT)
    pairs = [(i, i ^ bit) for i in range(size)]
    return lax.ppermute(in_rows(operand), CONTEXT, pairs).reshape(operand.shape)


def swap_tensor(operand):
    return lax.ppermute(in_rows(operand), TENSOR, [(0, 1), (1, 0)]).reshape(operand.shape)


def shift_fsdp(operand, step):
    size = lax.axis_size(FSDP)
    return lax.ppermute(operand, FSDP, [(i, (i + step) % size) for i in range(size)])


def paired():
    return lax.axis_size(TENSOR) == 2


def tensor_order(own, other, axis):
    first = lax.axis_index(TENSOR) == 0
    return jnp.concatenate(
        [jnp.where(first, own, other), jnp.where(first, other, own)], axis=axis
    )


def gather_tensor(own):
    if paired():
        return [own, swap_tensor(own)]
    return [lax.all_gather(own, TENSOR, axis=0, tiled=True)]


def term_shapes(rows, width):
    if paired():
        return [(rows // 2, width, jnp.float32), (rows // 2, width, LOW)]
    return [(rows, width, LOW)]


def split_terms(total):
    return own_and_other(total) if paired() else [total]


def sum_tensor(terms):
    if paired():
        return terms[0] + wide(swap_tensor(terms[1]))
    return wide(lax.psum_scatter(terms[0], TENSOR, scatter_dimension=0, tiled=True))


def columns_of(operand):
    parts = jnp.split(operand, lax.axis_size(TENSOR), axis=-1)
    if paired():
        first = lax.axis_index(TENSOR) == 0
        return [jnp.where(first, parts[0], parts[1]), jnp.where(first, parts[1], parts[0])]
    return parts


def join_columns(parts):
    if paired():
        return tensor_order(parts[0], parts[1], -1)
    return jnp.concatenate(parts, axis=-1)


def gather_fsdp_small(own):
    size = lax.axis_size(FSDP)
    place = lax.axis_index(FSDP)
    out = jnp.zeros((size,) + own.shape, own.dtype)
    out = lax.dynamic_update_index_in_dim(out, own, place, 0)
    for step in range(1, size):
        out = lax.dynamic_update_index_in_dim(
            out, shift_fsdp(own, step), (place - step + size) % size, 0
        )
    return out


def sum_fsdp_small(parts):
    size = lax.axis_size(FSDP)
    place = lax.axis_index(FSDP)
    total = lax.dynamic_index_in_dim(parts, place, 0, keepdims=False)
    for step in range(1, size):
        part = lax.dynamic_index_in_dim(parts, (place + step) % size, 0, keepdims=False)
        total = total + shift_fsdp(part, step)
    return total


def sum_context(total):
    for bit in (CORE, CHIP):
        total = total + swap_context(total, bit)
    return total


def gather_context(own):
    parts = [(0, own)]
    for bit in (CHIP, CORE):
        parts = parts + [(offset ^ bit, swap_context(part, bit)) for offset, part in parts]
    return parts


def multiply(body, lefts, rights, turned, extras, outs, after, tile=512):
    width = outs[0][1]
    tile = min(tile, width)
    counts = [len(lefts), len(rights), len(extras)]
    first, second, third = counts[0], sum(counts[:2]), sum(counts)

    def kernel(*refs):
        results, token_ref = refs[-len(outs) - 1 : -1], refs[-1]
        mark(token_ref)
        values = [ref[...] for ref in refs[:third]]
        for result, value in zip(
            results, body(values[:first], values[first:second], values[second:third])
        ):
            result[...] = value.astype(result.dtype)

    def column_block(rows):
        return pl.BlockSpec((rows, tile), lambda j: (0, j))

    def right_block(right):
        if turned:
            return pl.BlockSpec((tile, right.shape[1]), lambda j: (j, 0))
        return column_block(right.shape[0])

    flops = 2 * sum(right.size for right in rights) * outs[0][0]
    return pl.pallas_call(
        kernel,
        grid=(pl.cdiv(width, tile),),
        in_specs=[pl.BlockSpec(left.shape, lambda j: (0, 0)) for left in lefts]
        + [right_block(right) for right in rights]
        + [column_block(extra.shape[0]) for extra in extras]
        + [FREE] * len(after),
        out_specs=[column_block(rows) for rows, _, _ in outs] + [TOKEN_SPEC],
        out_shape=[jax.ShapeDtypeStruct((rows, wide_by), kind) for rows, wide_by, kind in outs]
        + [TOKEN],
        compiler_params=vmem(40),
        cost_estimate=cost(flops, 2 * sum(right.size for right in rights)),
    )(*lefts, *rights, *extras, *after)


def stacked(pieces, right, dim):
    parts = [contract(piece, right, 1, dim) for piece in pieces]
    return parts[0] if len(parts) == 1 else jnp.concatenate(parts, axis=0)


def own_and_other(total):
    rows = total.shape[0] // 2
    return [total[:rows], total[rows:]]


GELU_SCALE, GELU_CUBE = math.sqrt(2.0 / math.pi), 0.044715


def gelu(value):
    return 0.5 * value * (1.0 + jnp.tanh(GELU_SCALE * (value + GELU_CUBE * value**3)))


def gelu_slope(value):
    bend = jnp.tanh(GELU_SCALE * (value + GELU_CUBE * value**3))
    slope = GELU_SCALE * (1.0 + 3.0 * GELU_CUBE * value * value)
    return 0.5 * (1.0 + bend) + 0.5 * value * (1.0 - bend * bend) * slope


def meet_core():
    place = lax.axis_index(CONTEXT)
    other = {CONTEXT: place + 1 - 2 * (place % 2)}
    barrier = pltpu.get_barrier_semaphore()
    pl.semaphore_signal(barrier, inc=1, device_id=other, device_id_type=MESH)
    pl.semaphore_wait(barrier, 1)
    return other


def share_kernel(count, widths, *refs):
    sources, outs = refs[:count], refs[-count // 2 * widths - 4 :]
    targets, token_ref = outs[: count // 2 * widths], outs[-4]
    local_sem, send_sem, recv_sem = outs[-3:]
    mark(token_ref)
    place = lax.axis_index(CONTEXT)
    other = meet_core()
    copies = []
    for source_at in range(count):
        part, chip = source_at // 2, source_at % 2
        slot = (place + CHIP * chip) % 4
        for index in range(widths):
            sem = source_at * widths + index
            source = sources[source_at].at[:, index]
            target = targets[part * widths + index].at[:, slot]
            remote = pltpu.make_async_remote_copy(
                src_ref=source,
                dst_ref=target,
                send_sem=send_sem.at[sem],
                recv_sem=recv_sem.at[sem],
                device_id=other,
                device_id_type=MESH,
            )
            remote.start()
            own = pltpu.make_async_copy(source, target, local_sem.at[sem])
            own.start()
            copies += [remote, own]
    for copy in copies:
        copy.wait()


def share_core(pieces, after, ident):
    along, widths, rows, width = pieces[0].shape
    count = len(pieces)
    size = lax.axis_size(CONTEXT)
    total = count // 2 * widths
    shape = jax.ShapeDtypeStruct((along, size, rows, width), LOW)
    outs = pl.pallas_call(
        lambda *refs: share_kernel(count, widths, *refs),
        in_specs=[WHOLE] * count + [FREE] * len(after),
        out_specs=[IN_HBM] * total + [WHOLE],
        out_shape=[shape] * total + [TOKEN],
        scratch_shapes=[pltpu.SemaphoreType.DMA((count * widths,))] * 3,
        compiler_params=pltpu.CompilerParams(
            collective_id=ident, has_side_effects=True, vmem_limit_bytes=40 * MIB
        ),
        cost_estimate=cost(0, 6 * count * pieces[0].size * 2),
    )(*pieces, *after)
    held = [out.reshape(along * size * rows, width) for out in outs[:-1]]
    return [held[part * widths : (part + 1) * widths] for part in range(count // 2)], outs[-1]


def pack_of(shards):
    return jnp.stack([low(shard) for shard in shards], axis=0)


def gather_fsdp(shards, after):
    return lax.all_gather(gate(pack_of(shards), after), FSDP, axis=0, tiled=False)


def across(along, spread, after):
    along = gate(along, after) if after else along
    parts = [along, swap_context(along, CHIP)]
    if not spread:
        return parts
    if paired():
        first = swap_tensor(along)
        parts[1] = gate(parts[1], (first,))
        return parts + [first, swap_tensor(parts[1])]
    many = [lax.all_gather(part, TENSOR, axis=0) for part in parts]
    return [part[i] for i in range(lax.axis_size(TENSOR)) for part in many]


class Order:
    def __init__(self):
        self.after = ()
        self.count = 0

    def ident(self):
        self.count += 1
        return self.count - 1

    def need(self, *operands):
        self.after = self.after + operands

    def put(self, outs):
        *outs, token = outs
        self.after = (token,)
        return outs

    def multiply(self, body, lefts, rights, turned, extras, outs, tile=512):
        return self.put(multiply(body, lefts, rights, turned, extras, outs, self.after, tile))


def grad_kernel(which, spread, tile, counts, waits, *refs):
    count = sum(counts)
    lefts, rights = refs[:count], refs[count : count + len(which)]
    outs = refs[count + len(which) + waits :]
    kept, given = outs[: max(spread, 1)], outs[max(spread, 1) : 2 * max(spread, 1)]
    token_ref = outs[2 * max(spread, 1)]
    turned, cut, sent, came, send_sem, recv_sem = outs[2 * max(spread, 1) + 1 :]
    mark(token_ref)
    other = meet_core()
    place = lax.axis_index(CONTEXT)
    tiles = rights[0].shape[1] // tile
    rows = cut.shape[3]
    along = lax.axis_size(FSDP)
    block = rows // along
    for index, pieces in enumerate(counts):
        start = sum(counts[:index])
        depth = 0
        for left in lefts[start : start + pieces]:
            turned[:, depth : depth + left.shape[0]] = left[...].astype(jnp.float32).T
            depth += left.shape[0]
        for core in range(2):
            for chip in range(2):
                at = (place // 2 + chip) % 2 * 2 + (place % 2 + core) % 2
                pieces = [
                    turned[pl.ds(pl.multiple_of((4 * z + at) * block, 8), block), :]
                    for z in range(along)
                ]
                cut[index, core, chip] = low(jnp.concatenate(pieces, axis=0))
    units = []
    for job, left in enumerate(which):
        for chip in range(2):
            out = (kept, given)[chip]
            out = out[job % spread].at[job // spread] if spread else out[0].at[job]
            units.append((left, rights[job], chip, out))

    def columns(index):
        if isinstance(index, int):
            return pl.ds(index * tile, tile)
        return pl.ds(pl.multiple_of(index * tile, tile), tile)

    def copy(unit, index):
        sem = unit * tiles + index
        return pltpu.make_async_remote_copy(
            src_ref=sent.at[unit, index],
            dst_ref=came.at[unit, index],
            send_sem=send_sem.at[sem],
            recv_sem=recv_sem.at[sem],
            device_id=other,
            device_id_type=MESH,
        )

    def each(step):
        if tiles == 1:
            step(0)
        else:
            lax.fori_loop(0, tiles, lambda index, carry: (step(index), carry)[1], 0)

    for unit, (left, right, chip, out) in enumerate(units):

        def give(index, unit=unit, left=left, right=right, chip=chip):
            sent[unit, index] = low(contract(cut[left, 1, chip], right[:, columns(index)], 1, 0))
            copy(unit, index).start()

        each(give)
    for unit, (left, right, chip, out) in enumerate(units):

        def keep(index, unit=unit, left=left, right=right, chip=chip, out=out):
            term = contract(cut[left, 0, chip], right[:, columns(index)], 1, 0)
            copy(unit, index).wait_recv()
            out[:, columns(index)] = low(term + wide(came[unit, index]))

        each(keep)
    for unit in range(len(units)):

        def done(index, unit=unit):
            copy(unit, index).wait_send()

        each(done)


def grad_core(lefts, rights, which, spread, after, ident):
    depth, width = rights[0].shape
    counts = [len(pieces) for pieces in lefts]
    lefts = [piece for pieces in lefts for piece in pieces]
    features = lefts[0].shape[1]
    rows = features // 4
    jobs = len(which)
    count = max(spread, 1)
    tile = width
    for candidate in (512, 384):
        if width > 1408 and width % candidate == 0:
            tile = candidate
            break
    tiles = width // tile
    shape = jax.ShapeDtypeStruct((jobs // count, rows, width), LOW)
    outs = pl.pallas_call(
        lambda *refs: grad_kernel(which, spread, tile, counts, len(after), *refs),
        in_specs=[WHOLE] * (len(lefts) + jobs) + [FREE] * len(after),
        out_specs=[WHOLE] * (2 * count + 1),
        out_shape=[shape] * (2 * count) + [TOKEN],
        scratch_shapes=[
            pltpu.VMEM((features, depth), jnp.float32),
            pltpu.VMEM((len(counts), 2, 2, rows, depth), LOW),
            pltpu.VMEM((2 * jobs, tiles, rows, tile), LOW),
            pltpu.VMEM((2 * jobs, tiles, rows, tile), LOW),
            pltpu.SemaphoreType.DMA((2 * jobs * tiles,)),
            pltpu.SemaphoreType.DMA((2 * jobs * tiles,)),
        ],
        compiler_params=pltpu.CompilerParams(
            collective_id=ident, has_side_effects=True, vmem_limit_bytes=56 * MIB
        ),
        cost_estimate=cost(8 * jobs * rows * width * depth, 6 * jobs * width * rows),
    )(*lefts, *rights, *after)
    if spread:
        return list(outs[:count]), list(outs[count:-1]), outs[-1]
    return outs


def sum_parts(kept, given, order):
    if paired():
        pairs = [(kept[0], swap_tensor(kept[1])), (given[0], swap_tensor(given[1]))]
        return order.put(add_pairs(pairs, 0, order.after))
    return [
        lax.psum_scatter(jnp.stack(parts), TENSOR, scatter_dimension=0, tiled=False)
        for parts in (kept, given)
    ]


def sum_rest(kept, came, order):
    (total,) = order.put(add_pairs([(kept, came)], lax.axis_size(FSDP), order.after))
    return lax.psum_scatter(total, FSDP, scatter_dimension=0, tiled=False)


def sum_text(total):
    place = lax.axis_index(CONTEXT)
    steps = [
        (lambda operand: swap_context(operand, CORE), place % 2),
        (lambda operand: swap_context(operand, CHIP), place // 2),
    ]
    if paired():
        steps.append((swap_tensor, lax.axis_index(TENSOR)))
    for swap, bit in steps:
        half = total.shape[0] // 2
        kept = lax.dynamic_slice_in_dim(total, bit * half, half, axis=0)
        given = lax.dynamic_slice_in_dim(total, (1 - bit) * half, half, axis=0)
        total = low(wide(kept) + wide(swap(given)))
    if not paired():
        total = lax.psum(total, TENSOR)
    for swap, bit in reversed(steps):
        other = swap(total)
        first = bit == 0
        total = jnp.concatenate(
            [jnp.where(first, total, other), jnp.where(first, other, total)], axis=0
        )
    return total


def per_token(operand, rows):
    seqs, _, width = operand.shape
    return jnp.broadcast_to(operand, (seqs, rows // seqs, width)).reshape(rows, width)


def per_sequence(operand, seqs):
    return operand.reshape(seqs, -1, operand.shape[-1]).sum(axis=1)


def layer_forward(residual, skip_rows, modulation, text, tables, weights, order, steps):
    rows, features = residual.shape
    parts = lax.axis_size(TENSOR)
    every = rows * parts
    seqs = modulation[0].shape[0]
    shift_a, scale_a, gate_a, shift_m, scale_m, gate_m = [
        per_token(piece, rows) for piece in modulation
    ]
    cos, sin = tables
    kept = SimpleNamespace()
    kept.concat = jnp.concatenate([residual, wide(skip_rows)], axis=-1)
    kept.concat_low = low(layer_norm(kept.concat))
    width = weights.skip[0].shape[1]
    skipped = order.multiply(
        lambda lefts, rights, _: [contract(lefts[0], right, 1, 0) for right in rights],
        [kept.concat_low],
        weights.skip,
        False,
        [],
        [(rows, width, LOW)] * parts,
    )
    after_skip = wide(join_columns(skipped))
    kept.after_skip = after_skip
    kept.attn_all = gather_tensor(low(layer_norm(after_skip) * (1.0 + scale_a) + shift_a))
    steps.skipped()
    kept.query_raw, kept.key_raw, value_low = order.multiply(
        lambda lefts, rights, _: [stacked(lefts, right, 0) for right in rights],
        kept.attn_all,
        [weights.query, weights.key, weights.value],
        False,
        [],
        [(every, width, jnp.float32)] * 2 + [(every, width, LOW)],
    )
    blocks = (parts, seqs, rows // seqs, width)
    query_low, key_low = order.put(turn(kept.query_raw, kept.key_raw, cos, sin, order.after))
    kept.query_low = query_low.reshape(blocks)
    kept.keys = [part.reshape(blocks) for _, part in gather_context(key_low)]
    kept.values = [part.reshape(blocks) for _, part in gather_context(value_low)]
    steps.turned()
    attn_low, kept.attn_lse = attend(kept.query_low, kept.keys, kept.values, order.after)
    order.after = (kept.attn_lse,)
    kept.attn_low = attn_low.reshape(-1, width)
    terms = order.multiply(
        lambda lefts, rights, _: split_terms(contract(lefts[0], rights[0], 1, 1)),
        [kept.attn_low],
        [weights.attn_out],
        True,
        [],
        term_shapes(every, features),
    )
    kept.attn_branch = sum_tensor(terms)
    steps.attended()
    kept.after_attn = after_skip + gate_a * kept.attn_branch
    kept.cross_in = low(layer_norm(kept.after_attn))
    raws = order.multiply(
        lambda lefts, rights, _: [contract(lefts[0], right, 1, 0) for right in rights],
        [kept.cross_in],
        weights.cross_query,
        False,
        [],
        [(rows, width, jnp.float32)] * parts,
    )
    kept.cross_raw = [raw.reshape(blocks[1:]) for raw in raws]
    kept.cross_low = []
    for raw, key, value in zip(kept.cross_raw, text.keys, text.values):
        (out,) = order.put(cross(raw, key, value, text.count, order.after))
        kept.cross_low.append(out.reshape(rows, width))
    (kept.after_cross,) = order.multiply(
        lambda lefts, rights, extras: [
            sum((contract(left, right, 1, 1) for left, right in zip(lefts, rights)), extras[0])
        ],
        kept.cross_low,
        weights.cross_out,
        True,
        [kept.after_attn],
        [(rows, features, jnp.float32)],
    )
    after_cross = kept.after_cross
    kept.mlp_all = gather_tensor(low(layer_norm(after_cross) * (1.0 + scale_m) + shift_m))
    steps.crossed()

    def raise_and_bend(lefts, rights, _):
        upward = stacked(lefts, rights[0], 0)
        return [upward, gelu(upward)]

    hidden = weights.up.shape[1]
    kept.upward, kept.hidden_low = order.multiply(
        raise_and_bend,
        kept.mlp_all,
        [weights.up],
        False,
        [],
        [(every, hidden, jnp.float32), (every, hidden, LOW)],
    )
    steps.raised()
    terms = order.multiply(
        lambda lefts, rights, _: split_terms(contract(lefts[0], rights[0], 1, 1)),
        [kept.hidden_low],
        [weights.down],
        True,
        [],
        term_shapes(every, features),
    )
    kept.mlp_branch = sum_tensor(terms)
    steps.lowered()
    return after_cross + gate_m * kept.mlp_branch, kept


def layer_backward(grad_res, kept, weights, modulation, tables, text, text_low, order, earlier):
    rows, features = grad_res.shape
    parts = lax.axis_size(TENSOR)
    every = rows * parts
    seqs = modulation[0].shape[0]
    shift_a, scale_a, gate_a, shift_m, scale_m, gate_m = [
        per_token(piece, rows) for piece in modulation
    ]
    cos, sin = tables
    reduced = SimpleNamespace()

    def product(lefts, rights, which, spread):
        outs = order.put(grad_core(lefts, rights, which, spread, order.after, order.ident()))
        return outs if spread else (outs[0], swap_context(outs[1], CHIP))

    mlp_grad = gather_tensor(low(gate_m * grad_res))
    earlier.start()
    grad_gate_m = per_sequence(grad_res * kept.mlp_branch, seqs)
    (up_grad,) = order.multiply(
        lambda lefts, rights, extras: [stacked(lefts, rights[0], 0) * gelu_slope(extras[0])],
        mlp_grad,
        [weights.down],
        False,
        [kept.upward],
        [(every, kept.upward.shape[1], LOW)],
    )
    terms = order.multiply(
        lambda lefts, rights, _: split_terms(contract(lefts[0], rights[0], 1, 1)),
        [up_grad],
        [weights.up],
        True,
        [],
        term_shapes(every, features),
    )
    mlp_in_grad = sum_tensor(terms)
    order.need(*earlier.sums())
    down = product([mlp_grad], [kept.hidden_low], (0,), 0)
    earlier.first()
    up = product([kept.mlp_all], [up_grad], (0,), 0)
    grad_shift_m = per_sequence(mlp_in_grad, seqs)
    grad_scale_m = per_sequence(mlp_in_grad * layer_norm(kept.after_cross), seqs)
    grad_res = grad_res + layer_norm_back(kept.after_cross, mlp_in_grad * (1.0 + scale_m))

    cross_grad = low(grad_res)
    width = weights.cross_out[0].shape[1]
    out_grads = order.multiply(
        lambda lefts, rights, _: [contract(lefts[0], right, 1, 0) for right in rights],
        [cross_grad],
        weights.cross_out,
        False,
        [],
        [(rows, width, LOW)] * parts,
    )
    cross_q, text_key_grad, text_value_grad = [], [], []
    for part, out_grad in enumerate(out_grads):
        raw = kept.cross_raw[part]
        query_grad, key_grad, value_grad = order.put(
            cross_back(
                raw,
                text.raws[part],
                text.keys[part],
                text.values[part],
                out_grad.reshape(raw.shape),
                text.count,
                order.after,
            )
        )
        cross_q.append(query_grad.reshape(rows, width))
        text_key_grad.append(key_grad.reshape(-1, width))
        text_value_grad.append(value_grad.reshape(-1, width))
    (cross_in_grad,) = order.multiply(
        lambda lefts, rights, _: [
            sum(contract(left, right, 1, 1) for left, right in zip(lefts, rights))
        ],
        cross_q,
        weights.cross_query,
        True,
        [],
        [(rows, features, jnp.float32)],
    )
    grad_res = grad_res + layer_norm_back(kept.after_attn, cross_in_grad)

    attn_grad = gather_tensor(low(gate_a * grad_res))
    earlier.second()
    grad_gate_a = per_sequence(grad_res * kept.attn_branch, seqs)
    crossed = product(
        [[cross_grad], [kept.cross_in]],
        kept.cross_low + cross_q,
        (0,) * parts + (1,) * parts,
        parts,
    )
    texts = product([[text_low]], text_key_grad + text_value_grad, (0,) * (2 * parts), parts)
    (out_grad,) = order.multiply(
        lambda lefts, rights, _: [stacked(lefts, rights[0], 0)],
        attn_grad,
        [weights.attn_out],
        False,
        [],
        [(every, width, LOW)],
    )
    blocks = kept.query_low.shape
    order.need(*earlier.more())
    query_grad, key_parts, value_parts = order.put(
        attend_back(
            kept.query_low,
            kept.query_raw.reshape(blocks),
            out_grad.reshape(blocks),
            kept.attn_lse,
            cos.reshape(blocks),
            sin.reshape(blocks),
            kept.keys,
            kept.values,
            order.after,
        )
    )
    query_grad = query_grad.reshape(-1, width)

    key_parts, value_parts = [
        [piece.reshape(1, -1, width) for piece in pieces] for pieces in (key_parts, value_parts)
    ]
    near = [
        (pieces[place], swap_context(pieces[place + 2], CORE))
        for pieces in (key_parts, value_parts)
        for place in range(2)
    ]
    reduced.down = sum_rest(*down, order)
    key_near, key_far, value_near, value_far = order.put(add_pairs(near, 0, order.after))
    whole = [
        (key_near, swap_context(key_far, CHIP)),
        (value_near, swap_context(value_far, CHIP)),
    ]
    reduced.up = sum_rest(*up, order)
    (text_part,) = order.multiply(
        lambda lefts, rights, _: [
            sum(contract(left, right, 1, 1) for left, right in zip(lefts, rights))
        ],
        text_key_grad + text_value_grad,
        weights.text_key + weights.text_value,
        True,
        [],
        [(text_low.shape[0], text_low.shape[1], jnp.float32)],
        256,
    )
    crossed = sum_parts(*crossed, order)
    earlier.third()
    key_grad, value_grad = order.put(add_pairs(whole, 0, order.after))
    crossed = (crossed[0], swap_context(gate(crossed[1], order.after), CHIP))
    (key_grad,) = order.put(turn_back(key_grad[0], kept.key_raw, cos, sin, order.after))
    value_grad = value_grad[0]
    terms = order.multiply(
        lambda lefts, rights, _: split_terms(
            sum(contract(left, right, 1, 1) for left, right in zip(lefts, rights))
        ),
        [query_grad, key_grad, value_grad],
        [weights.query, weights.key, weights.value],
        True,
        [],
        term_shapes(every, features),
    )
    attn_in_grad = sum_tensor(terms)
    attended = product(
        [attn_grad, kept.attn_all],
        [kept.attn_low, query_grad, key_grad, value_grad],
        (0, 1, 1, 1),
        0,
    )
    texts = sum_parts(*texts, order)
    texts = (texts[0], swap_context(texts[1], CHIP))
    grad_shift_a = per_sequence(attn_in_grad, seqs)
    grad_scale_a = per_sequence(attn_in_grad * layer_norm(kept.after_skip), seqs)
    grad_res = grad_res + layer_norm_back(kept.after_skip, attn_in_grad * (1.0 + scale_a))

    skip_grad = columns_of(low(grad_res))
    (concat_grad,) = order.multiply(
        lambda lefts, rights, _: [
            sum(contract(left, right, 1, 1) for left, right in zip(lefts, rights))
        ],
        skip_grad,
        weights.skip,
        True,
        [],
        [(rows, 2 * features, jnp.float32)],
    )
    later = SimpleNamespace()

    def start():
        later.skipped = product([[kept.concat_low]], skip_grad, (0,) * parts, parts)
        reduced.cross = sum_rest(*crossed, order)

    def first():
        reduced.attention = sum_rest(*attended, order)

    def second():
        reduced.text = sum_rest(*texts, order)
        kept, given = sum_parts(*later.skipped, order)
        later.skipped = (kept, swap_context(given, CHIP))

    def third():
        reduced.skip = sum_rest(*later.skipped, order)

    later.start, later.first, later.second, later.third = start, first, second, third
    concat_grad = layer_norm_back(kept.concat, concat_grad)
    mod_grad = jnp.concatenate(
        [grad_shift_a, grad_scale_a, grad_gate_a, grad_shift_m, grad_scale_m, grad_gate_m], axis=-1
    )
    mod_columns = columns_of(mod_grad)
    if paired():
        mod_columns = mod_columns[0] + swap_tensor(mod_columns[1])
    else:
        mod_columns = lax.psum_scatter(
            jnp.stack(mod_columns), TENSOR, scatter_dimension=0, tiled=False
        )
    mod_all = gather_fsdp_small(sum_context(mod_columns))
    mod_all = mod_all.reshape(-1, mod_all.shape[-1])
    later.sums = lambda: (reduced.down, reduced.up)
    later.more = lambda: (reduced.cross, reduced.attention)
    return concat_grad[:, :features], concat_grad[:, features:], mod_all, text_part, reduced, later


def shards(
    latents,
    skip_inputs,
    text_states,
    condition,
    positions,
    cotangent,
    *tensors,
):
    masters, momenta, averages = tensors[:7], tensors[7:14], tensors[14:]
    (
        skip_weight,
        mod_weight,
        proj_weight,
        output_weight,
        text_weight,
        up_weight,
        down_weight,
    ) = masters
    layers = skip_weight.shape[0]
    along = lax.axis_size(FSDP)
    size = lax.axis_size(CONTEXT)
    parts = lax.axis_size(TENSOR)
    seqs, tokens = latents.shape[0], latents.shape[1]
    text_count = text_states.shape[1]
    every = range(layers)

    def cross_of(layer):
        return [proj_weight[layer, :, 3], output_weight[layer, 1].T]

    def attention_of(layer):
        return [proj_weight[layer, :, j] for j in range(3)] + [output_weight[layer, 0].T]

    order = Order()
    weights = [SimpleNamespace() for _ in every]
    skip_along = gather_fsdp_small(pack_of([skip_weight[0]]))
    arrived = (skip_along,)
    skip_parts = across(skip_along, True, ())
    started = (skip_parts[1],)
    cross_along = [gather_fsdp_small(gate(pack_of(cross_of(0)), arrived))]
    skips = [skip_along]
    for layer in every[1:]:
        skips.append(gather_fsdp_small(gate(pack_of([skip_weight[layer]]), started)))
        cross_along.append(gather_fsdp_small(gate(pack_of(cross_of(layer)), started)))
    attention = [gather_fsdp(attention_of(0), arrived)]
    text_along = gather_fsdp([text_weight[i, :, j] for i in every for j in range(2)], arrived)
    ups = [gather_fsdp([up_weight[0]], arrived)]
    downs = [gather_fsdp([down_weight[0].T], arrived)]
    for layer in every[1:]:
        attention.append(gather_fsdp(attention_of(layer), started))
        ups.append(gather_fsdp([up_weight[layer]], started))
        downs.append(gather_fsdp([down_weight[layer].T], started))

    attention_parts, cross_parts, up_parts, down_parts = {}, {}, {}, {}
    skip_parts = {0: skip_parts}

    def hold_skip(layer):
        (held,) = order.put(share_core(skip_parts[layer], order.after, order.ident()))
        weights[layer].skip = [part[0] for part in held]

    def hold_attention(layer):
        (held,) = order.put(share_core(attention_parts[layer], order.after, order.ident()))
        place = weights[layer]
        place.query, place.key, place.value, place.attn_out = held[0]

    def hold_cross(layer):
        (held,) = order.put(share_core(cross_parts[layer], order.after, order.ident()))
        weights[layer].cross_query = [part[0] for part in held]
        weights[layer].cross_out = [part[1] for part in held]

    def hold_up(layer):
        (held,) = order.put(share_core(up_parts[layer], order.after, order.ident()))
        weights[layer].up = held[0][0]

    def hold_down(layer):
        (held,) = order.put(share_core(down_parts[layer], order.after, order.ident()))
        weights[layer].down = held[0][0]

    padded = -(-text_count // 128) * 128
    text_low = jnp.pad(text_states, ((0, 0), (0, padded - text_count), (0, 0)))
    text_low = text_low.reshape(seqs * padded, -1)
    texts = [SimpleNamespace(count=text_count) for _ in every]

    def hold_text():
        (held,) = order.put(share_core(text_parts[0], order.after, order.ident()))
        for layer in every:
            weights[layer].text_key = [part[2 * layer] for part in held]
            weights[layer].text_value = [part[2 * layer + 1] for part in held]

    def read_text(layer):
        text = texts[layer]
        place = weights[layer]
        width = place.text_key[0].shape[1]
        outs = order.multiply(
            lambda lefts, rights, _: [contract(lefts[0], right, 1, 0) for right in rights],
            [text_low],
            place.text_key + place.text_value,
            False,
            [],
            [(seqs * padded, width, jnp.float32)] * parts + [(seqs * padded, width, LOW)] * parts,
            256,
        )
        blocks = (seqs, padded, width)
        keys = [order.put(root(raw, order.after))[0] for raw in outs[:parts]]
        text.raws = [raw.reshape(blocks) for raw in outs[:parts]]
        text.keys = [key.reshape(blocks) for key in keys]
        text.values = [value.reshape(blocks) for value in outs[parts:]]

    text_parts = {}
    attention_parts[0] = across(attention[0], False, (skip_parts[0][-1],))
    order.need(cross_along[0])
    hold_skip(0)

    def steps_of(layer):
        steps = SimpleNamespace()
        coming = layer + 1 if layer + 1 < layers else None

        def skipped():
            if not layer:
                text_parts[0] = across(text_along, True, order.after)
            hold_attention(layer)

        def turned():
            if layer:
                read_text(layer)
            else:
                cross_parts[layer] = across(cross_along[layer], True, order.after)

        def attended():
            if layer:
                down_parts[layer] = across(downs[layer], False, order.after)
                hold_up(layer)
            else:
                up_parts[layer] = across(ups[layer], False, order.after)
                hold_text()
                down_parts[layer] = across(downs[layer], False, order.after)
                read_text(layer)
                if coming:
                    order.need(skips[coming])
            hold_cross(layer)
            if coming:
                skip_parts[coming] = across(skips[coming], True, order.after)

        def crossed():
            if not layer:
                hold_up(layer)
            if coming:
                attention_parts[coming] = across(attention[coming], False, order.after)
                order.need(cross_along[coming])

        def raised():
            hold_down(layer)
            if coming:
                cross_parts[coming] = across(cross_along[coming], True, order.after)

        def lowered():
            if coming:
                hold_skip(coming)
                up_parts[coming] = across(ups[coming], False, order.after)

        steps.skipped, steps.turned, steps.attended = skipped, turned, attended
        steps.crossed, steps.raised, steps.lowered = crossed, raised, lowered
        return steps

    cond_float = wide(condition)
    cond_silu, silu_pull = jax.vjp(jax.nn.silu, cond_float)
    cond_all = gather_fsdp_small(low(cond_silu)).reshape(along * seqs, cond_float.shape[1])
    rows = mod_weight.shape[1]
    place = lax.axis_index(FSDP) * size + lax.axis_index(CONTEXT)
    cond_rows = lax.dynamic_slice_in_dim(cond_all, place * rows, rows, axis=1)
    mod_low = low(mod_weight)
    mod_part = contract(cond_rows, mod_low, 1, 1)
    mod_part = gate(mod_part, arrived).reshape((along, seqs) + mod_part.shape[1:])
    mod_part = sum_fsdp_small(mod_part)
    mod_part = low(sum_context(gate(mod_part, (skip_parts[0][-1],))))
    if paired():
        mod_full = tensor_order(mod_part, swap_tensor(mod_part), -1)
    else:
        mod_full = lax.all_gather(mod_part, TENSOR, axis=2, tiled=True)
    modulations = [
        jnp.split(wide(mod_full[:, layer])[:, None, :], 6, axis=-1) for layer in every
    ]

    quarter = HD // 4
    frequency = ROPE_BASE ** (-jnp.arange(quarter, dtype=jnp.float32) / quarter)
    grid = positions.reshape(seqs, 2, parts, tokens)
    if paired():
        mine = lax.axis_index(TENSOR)
        grid = jnp.concatenate(
            [
                lax.dynamic_slice_in_dim(grid, mine, 1, axis=2),
                lax.dynamic_slice_in_dim(grid, 1 - mine, 1, axis=2),
            ],
            axis=2,
        )
    grid = wide(grid.transpose(2, 0, 3, 1).reshape(parts * seqs * tokens, 2))
    row_angle = grid[:, :1] * frequency
    col_angle = grid[:, 1:] * frequency
    cos = jnp.concatenate([jnp.cos(row_angle)] * 2 + [jnp.cos(col_angle)] * 2, axis=-1)
    sin = jnp.concatenate(
        [-jnp.sin(row_angle), jnp.sin(row_angle), -jnp.sin(col_angle), jnp.sin(col_angle)], axis=-1
    )
    tables = spread_heads(cos, sin, proj_weight.shape[-1])

    own = (seqs * tokens, latents.shape[-1])
    residual = wide(latents).reshape(own)
    stored = []
    for layer in every:
        residual, kept = layer_forward(
            residual,
            skip_inputs[layer].reshape(own),
            modulations[layer],
            texts[layer],
            tables,
            weights[layer],
            order,
            steps_of(layer),
        )
        stored.append(kept)
    block_output = low(residual).reshape(latents.shape)

    grad_res = wide(cotangent).reshape(own)
    cond_total = 0.0
    text_total = 0.0
    skip_grads = [None] * layers
    gradients = [None] * layers
    later = SimpleNamespace(
        start=lambda: None, first=lambda: None, second=lambda: None, third=lambda: None, sums=lambda: (), more=lambda: ()
    )
    for layer in reversed(every):
        grad_res, skip_grads[layer], mod_all, text_part, reduced, later = layer_backward(
            grad_res,
            stored[layer],
            weights[layer],
            modulations[layer],
            tables,
            texts[layer],
            text_low,
            order,
            later,
        )
        reduced.mod = jnp.einsum("bk,bc->kc", wide(cond_rows), mod_all, precision=PRECISE)
        cond_total = cond_total + jnp.einsum(
            "bc,kc->bk", mod_all, wide(mod_low[layer]), precision=PRECISE
        )
        text_total = text_total + text_part
        gradients[layer] = reduced
    later.start()
    later.first()
    later.second()
    later.third()
    gradients = [
        (
            wide(each.skip[0]),
            each.mod,
            wide(jnp.concatenate([each.attention[1:], each.cross[1:]], axis=0)).transpose(1, 0, 2),
            wide(jnp.stack([each.attention[0], each.cross[0]], axis=0)).transpose(0, 2, 1),
            wide(each.text).transpose(1, 0, 2),
            wide(each.up[0]),
            wide(each.down[0]).T,
        )
        for each in gradients
    ]
    text_sum = sum_text(low(text_total))
    text_sum = wide(text_sum).reshape(seqs, padded, -1)[:, :text_count]
    if paired():
        cond_total = cond_total + swap_tensor(cond_total)
    else:
        cond_total = lax.psum(cond_total, TENSOR)
    sent = cond_total.reshape(along, seqs, rows)
    here = lax.axis_index(FSDP)
    cond_sum = jnp.zeros((along, size, seqs, rows), jnp.float32)
    for step in range(along):
        part = lax.dynamic_index_in_dim(sent, (here + step) % along, 0, keepdims=False)
        if step:
            part = shift_fsdp(part, step)
        for offset, piece in gather_context(part):
            cond_sum = lax.dynamic_update_slice(
                cond_sum,
                piece[None, None],
                ((here - step + along) % along, lax.axis_index(CONTEXT) ^ offset, 0, 0),
            )
    cond_sum = cond_sum.transpose(2, 0, 1, 3).reshape(seqs, along * size * rows)
    condition_grad = silu_pull(cond_sum)[0]
    skips_grad = jnp.stack(skip_grads, axis=0).reshape(skip_inputs.shape)

    spreads = (
        (2 * D) ** (-0.5),
        D ** (-0.5),
        D ** (-0.5),
        (D // 16) ** (-0.5),
        DT ** (-0.5),
        D ** (-0.5),
        FF ** (-0.5),
    )
    tokens_total = seqs * along * tokens * size * parts
    new_weights = []
    new_momenta = []
    new_averages = []
    for index in range(len(masters)):
        gradient = jnp.stack([gradients[layer][index] for layer in every], axis=0)
        rate = RATE_FACTOR * spreads[index] / math.sqrt(tokens_total)
        moment_new = MOMENTUM * momenta[index] + gradient
        weight_new = masters[index] - rate * (gradient + MOMENTUM * moment_new)
        new_weights.append(weight_new)
        new_momenta.append(moment_new)
        new_averages.append(
            AVERAGE_DECAY * averages[index] + (1.0 - AVERAGE_DECAY) * weight_new
        )
    return (
        block_output,
        grad_res.reshape(latents.shape),
        skips_grad,
        text_sum,
        condition_grad,
        *new_weights,
        *new_momenta,
        *new_averages,
    )


def solution(mesh):
    weight_specs = (
        P(None, (FSDP, CONTEXT), TENSOR),
        P(None, (FSDP, CONTEXT), TENSOR),
        P(None, (FSDP, CONTEXT), None, TENSOR),
        P(None, None, TENSOR, (FSDP, CONTEXT)),
        P(None, (FSDP, CONTEXT), None, TENSOR),
        P(None, (FSDP, CONTEXT), TENSOR),
        P(None, TENSOR, (FSDP, CONTEXT)),
    )
    in_specs = (
        P(FSDP, (CONTEXT, TENSOR), None),
        P(None, FSDP, (CONTEXT, TENSOR), None),
        P(FSDP, None, None),
        P(FSDP, None),
        P(FSDP, None, CONTEXT),
        P(FSDP, (CONTEXT, TENSOR), None),
    ) + weight_specs * 3
    out_specs = (
        P(FSDP, (CONTEXT, TENSOR), None),
        P(FSDP, (CONTEXT, TENSOR), None),
        P(None, FSDP, (CONTEXT, TENSOR), None),
        P(FSDP, None, None),
        P(FSDP, None),
    ) + weight_specs * 3
    return jax.shard_map(shards, mesh=mesh, in_specs=in_specs, out_specs=out_specs, check_vma=False)
```

profile of v0, /device:TPU:0, one launch (start us, length us, event | category | flops | bytes accessed | tf_op | source)
XLA Modules:
  0.0 1775.3 jit_solution(9881962770870311523)
XLA Ops:
  101.0 17.9 %collective-permute-done.7 = bf16[2,88,704]{2,1,0:T(8,128)(2,1)S(1)} collective-permute-done((bf16[2,88,704]{2,1,0:T(8,128)(2,1)S(1)}, bf16[2,88,704]{2,1,0:T(8,128)(2,1)S(1)}, u32[]{:S(2)}, u32[]{:S(2)}) %collective-permute-start.7) | collective-permute-done | bytes 247840 | tf_op jit(solution)/shard_map/ppermute | solution.py:494
  155.6 40.1 %collective-permute-done.19.refs_1_ = bf16[4,4,88,704]{3,2,1,0:T(8,128)(2,1)} collective-permute-done((bf16[4,4,88,704]{3,2,1,0:T(8,128)(2,1)}, bf16[4,4,88,704]{3,2,1,0:T(8,128)(2,1)}, u32[]{:S(2)}, u32[]{:S(2)}) %collective-permute-start.19) | collective-permute-done | bytes 1982496 | tf_op jit(solution)/shard_map/ppermute | solution.py:485
  231.0 38.4 %collective-permute-done.20 = bf16[64,8,704]{2,1,0:T(8,128)(2,1)} collective-permute-done((bf16[64,8,704]{2,1,0:T(8,128)(2,1)}, bf16[64,8,704]{2,1,0:T(8,128)(2,1)}, u32[]{:S(2)}, u32[]{:S(2)}) %collective-permute-start.20) | collective-permute-done | bytes 720928 | tf_op jit(solution)/shard_map/ppermute | solution.py:485
  288.1 19.2 %collective-permute-start.33 = (bf16[1,176,704]{2,1,0:T(8,128)(2,1)S(1)}, bf16[1,176,704]{2,1,0:T(8,128)(2,1)S(1)}, u32[]{:S(2)}, u32[]{:S(2)}) collective-permute-start(bf16[1,176,704]{2,1,0:T(8,128)(2,1)S(1)} %copy-done.401), channel_id=1, source_target_pairs={{0,8},{8,16},{16,24},{24,0},{1,9},{9,17},{17,25},{25,1},{2,10},{10... | collective-permute-start | bytes 743432 | tf_op jit(solution)/shard_map/ppermute | solution.py:494
  430.4 25.9 %collective-permute-done.43.refs_0_ = bf16[4,1,176,704]{3,2,1,0:T(8,128)(2,1)} collective-permute-done((bf16[4,1,176,704]{3,2,1,0:T(8,128)(2,1)}, bf16[4,1,176,704]{3,2,1,0:T(8,128)(2,1)}, u32[]{:S(2)}, u32[]{:S(2)}) %collective-permute-start.43) | collective-permute-done | bytes 991264 | tf_op jit(solution)/shard_map/ppermute | solution.py:485
  550.7 21.2 %collective-permute-done.47.refs_1_ = bf16[4,4,88,704]{3,2,1,0:T(8,128)(2,1)} collective-permute-done((bf16[4,4,88,704]{3,2,1,0:T(8,128)(2,1)}, bf16[4,4,88,704]{3,2,1,0:T(8,128)(2,1)}, u32[]{:S(2)}, u32[]{:S(2)}) %collective-permute-start.47) | collective-permute-done | bytes 1982496 | tf_op jit(solution)/shard_map/ppermute | solution.py:485
  603.3 17.8 %collective-permute-done.48 = bf16[64,8,704]{2,1,0:T(8,128)(2,1)} collective-permute-done((bf16[64,8,704]{2,1,0:T(8,128)(2,1)}, bf16[64,8,704]{2,1,0:T(8,128)(2,1)}, u32[]{:S(2)}, u32[]{:S(2)}) %collective-permute-start.48) | collective-permute-done | bytes 720928 | tf_op jit(solution)/shard_map/ppermute | solution.py:485
  621.1 16.8 collective-permute-done.51
  729.3 16.7 collective-permute-done.59.refs_1_
  912.8 21.9 %shard_map.536 = (bf16[2,2,128,704]{3,2,1,0:T(8,128)(2,1)}, bf16[2,2,128,704]{3,2,1,0:T(8,128)(2,1)}, bf16[2,2,128,704]{3,2,1,0:T(8,128)(2,1)}, bf16[2,2,128,704...) custom-call(bf16[2,2,128,704]{3,2,1,0:T(8,128)(2,1)} %bitcast.712, ...), custom_call_target="tpu_custom_call" | custom-call | flops 10737418 | bytes 14417 | tf_op jit(solution)/shard_map/pallas_call | solution.py:283
  975.1 22.6 %collective-permute-done.73.refs_3_ = bf16[2,352,704]{2,1,0:T(8,128)(2,1)S(1)} collective-permute-done((bf16[2,352,704]{2,1,0:T(8,128)(2,1)}, bf16[2,352,704]{2,1,0:T(8,128)(2,1)S(1)}, u32[]{:S(2)}, u32[]{:S(2)}) %collective-permute-start.73) | collective-permute-done | bytes 991264 | tf_op jit(solution)/shard_map/ppermute | solution.py:489
  1081.3 17.5 collective-permute-done.78.refs_1_
  1124.2 20.2 %shard_map.553 = (bf16[1,352,3072]{2,1,0:T(8,128)(2,1)}, bf16[1,352,3072]{2,1,0:T(8,128)(2,1)}, f32[8,128]{1,0:T(8,128)}) custom-call(bf16[256,1408]{1,0:T(8,128)(2,1)} %copy-done.106, bf16[256,1408]{1,0:T(8,128)(2,1)} %copy-done.231, bf16[512,3072]{1,0:T(8,128)(2,1)} %copy-done.47, f32[8,128]{1,0:T(8,128)} %copy-done.327, bf16[1,88,3072]{2,1,0:T(8,128)(2,1)} %bitcast.802, ...), custom_call_target="tpu_custom_call" | custom-call | flops 4429185 | bytes 6488 | tf_op jit(solution)/shard_map/pallas_call | solution.py:839
  1173.6 20.8 %shard_map.555 = (bf16[1,352,3072]{2,1,0:T(8,128)(2,1)}, bf16[1,352,3072]{2,1,0:T(8,128)(2,1)}, f32[8,128]{1,0:T(8,128)}) custom-call(bf16[256,1408]{1,0:T(8,128)(2,1)} %fusion.35.refs_0_, bf16[256,1408]{1,0:T(8,128)(2,1)} %collective-permute-done.36.refs_1_, bf16[512,3072]{1,0:T(8,128)(2,1)} %copy-done.48, f32[8,128]{1,0:T(8,128)} %copy-done.333), custom_call_target="tpu_custom_call" | custom-call | flops 4429185 | bytes 6488 | tf_op jit(solution)/shard_map/pallas_call | solution.py:839
  1239.3 17.7 shard_map.562
  1257.0 20.7 %shard_map.563 = (bf16[2,256,704]{2,1,0:T(8,128)(2,1)}, bf16[2,256,704]{2,1,0:T(8,128)(2,1)}, bf16[2,256,704]{2,1,0:T(8,128)(2,1)}, bf16[2,256,704]{2,1,0:T(8,128)(2,1)}, f32[8,128]{1,0:T(8,128)}) custom-call(bf16[768,1024]{1,0:T(8,128)(2,1)} %bitcast.597, bf16[768,704]{1,0:T(8,128)(2,1)} %bitcast.680, bf16[768,704]{1,0:T(8,128)(2,1)} %bitcast.684, ...), custom_call_target="tpu_custom_call" | custom-call | flops 4429185 | bytes 4325 | tf_op jit(solution)/shard_map/pallas_call | solution.py:839
  1283.2 21.9 %shard_map.565 = (bf16[2,2,128,704]{3,2,1,0:T(8,128)(2,1)}, bf16[2,2,128,704]{3,2,1,0:T(8,128)(2,1)}, bf16[2,2,128,704]{3,2,1,0:T(8,128)(2,1)}, bf16[2,2,128,704...) custom-call(bf16[2,2,128,704]{3,2,1,0:T(8,128)(2,1)} %bitcast.730, ...), custom_call_target="tpu_custom_call" | custom-call | flops 10737418 | bytes 14417 | tf_op jit(solution)/shard_map/pallas_call | solution.py:283
  1326.7 33.2 %collective-permute-done.96.refs_1_ = bf16[1,352,3072]{2,1,0:T(8,128)(2,1)S(1)} collective-permute-done((bf16[1,352,3072]{2,1,0:T(8,128)(2,1)}, bf16[1,352,3072]{2,1,0:T(8,128)(2,1)S(1)}, u32[]{:S(2)}, u32[]{:S(2)}) %collective-permute-start.96) | collective-permute-done | bytes 2162720 | tf_op jit(solution)/shard_map/ppermute | solution.py:485
  1400.0 16.2 collective-permute-done.92
  1431.2 18.5 %shard_map.575 = (bf16[4,352,704]{2,1,0:T(8,128)(2,1)}, bf16[4,352,704]{2,1,0:T(8,128)(2,1)}, f32[8,128]{1,0:T(8,128)}) custom-call(bf16[256,1408]{1,0:T(8,128)(2,1)} %copy-done.109, bf16[256,1408]{1,0:T(8,128)(2,1)} %copy-done.234, bf16[256,1408]{1,0:T(8,128)(2,1)} %copy-done.108, bf16[256,1408]{1,0:T(8,128)(2,1)} %copy-done.233, ...), custom_call_target="tpu_custom_call" | custom-call | flops 4060086 | bytes 5947 | tf_op jit(solution)/shard_map/pallas_call | solution.py:839
  1466.3 18.4 %shard_map.578 = (bf16[1,704,704]{2,1,0:T(8,128)(2,1)}, bf16[1,704,704]{2,1,0:T(8,128)(2,1)}, bf16[1,704,704]{2,1,0:T(8,128)(2,1)}, bf16[1,704,704]{2,1,0:T(8,128)(2,1)}, f32[8,128]{1,0:T(8,128)}) custom-call(bf16[256,2816]{1,0:T(8,128)(2,1)} %multiply_convert_fusion.1.refs_0_, bf16[256,704]{1,0:T(8,128)(2,1)} %copy-done.206, bf16[256,704]{1,0:T(8,128)(2,1)} %copy-done.205, ...), custom_call_target="tpu_custom_call" | custom-call | flops 2030043 | bytes 5947 | tf_op jit(solution)/shard_map/pallas_call | solution.py:839
  1500.9 39.6 %collective-permute-done.137.refs_1_ = bf16[4,352,704]{2,1,0:T(8,128)(2,1)} collective-permute-done((bf16[4,352,704]{2,1,0:T(8,128)(2,1)}, bf16[4,352,704]{2,1,0:T(8,128)(2,1)}, u32[]{:S(2)}, u32[]{:S(2)}) %collective-permute-start.137) | collective-permute-done | bytes 1982496 | tf_op jit(solution)/shard_map/ppermute | solution.py:485
  1629.0 21.6 %collective-permute-done.135.refs_3_ = bf16[1,704,704]{2,1,0:T(8,128)(2,1)} collective-permute-done((bf16[1,704,704]{2,1,0:T(8,128)(2,1)}, bf16[1,704,704]{2,1,0:T(8,128)(2,1)}, u32[]{:S(2)}, u32[]{:S(2)}) %collective-permute-start.135) | collective-permute-done | bytes 991264 | tf_op jit(solution)/shard_map/ppermute | solution.py:489
  1728.8 25.4 %reduce-scatter.25.cloned.1.call-done = bf16[1,4,88,704]{3,2,1,0:T(8,128)(2,1)} async-done(((bf16[4,4,88,704]{3,2,1,0:T(8,128)(2,1)}), bf16[1,4,88,704]{3,2,1,0:T(8,128)(2,1)}) %reduce-scatter.25.cloned.1.call-update) | async-done | bytes 495632 | tf_op jit(solution)/shard_map/reduce_scatter | solution.py:874
  (1571 shorter events, 1205.6 us)
Async XLA Ops:
  7.2 138.1 %all-gather.15.cloned.1.call-start = ((), (), s32[]{:S(2)}) async-start(), calls=%async_computation.24 | async-start | bytes 2703360 | tf_op jit(solution)/shard_map/all_gather | solution.py:707
  32.8 114.3 %all-gather.17.cloned.1.call-start = ((), (), s32[]{:S(2)}) async-start(), calls=%async_computation.25 | async-start | bytes 1966080 | tf_op jit(solution)/shard_map/all_gather | solution.py:707
  34.9 307.4 %all-gather.19.cloned.1.call-start = ((), (), s32[]{:S(2)}) async-start(), calls=%async_computation.26 | async-start | bytes 2703360 | tf_op jit(solution)/shard_map/all_gather | solution.py:707
  54.5 311.8 %all-gather.21.cloned.1.call-start = ((), (), s32[]{:S(2)}) async-start(), calls=%async_computation.27 | async-start | bytes 2703360 | tf_op jit(solution)/shard_map/all_gather | solution.py:707
  62.2 459.4 %all-gather.23.cloned.1.call-start = ((), (), s32[]{:S(2)}) async-start(), calls=%async_computation.28 | async-start | bytes 2703360 | tf_op jit(solution)/shard_map/all_gather | solution.py:707
  119.0 483.4 %all-gather.25.cloned.1.call-start = ((), (), s32[]{:S(2)}) async-start(), calls=%async_computation.29 | async-start | bytes 2703360 | tf_op jit(solution)/shard_map/all_gather | solution.py:707
  331.7 346.2 %all-gather.27.cloned.1.call-start = ((), (), s32[]{:S(2)}) async-start(), calls=%async_computation.30 | async-start | bytes 2703360 | tf_op jit(solution)/shard_map/all_gather | solution.py:707
  342.3 127.5 %collective-permute-start.37 = (bf16[4,1,88,3072]{3,2,1,0:T(8,128)(2,1)}, bf16[4,1,88,3072]{3,2,1,0:T(8,128)(2,1)}, u32[]{:S(2)}, u32[]{:S(2)}) collective-permute-start(bf16[4,1,88,3072]{3,2,1,0:T(8,128)(2,1)} %shard_map.488.refs_0_), channel_id=1, source_target_pairs={{0,4},{2,6},{4,0},{6,2},{1,5},{3,7},{5,1},{7,3},{8,12},{10,14},{12... | collective-permute-start | bytes 6488072 | tf_op jit(solution)/shard_map/ppermute | solution.py:485
  366.3 129.8 %collective-permute-start.41 = (bf16[4,1,88,3072]{3,2,1,0:T(8,128)(2,1)}, bf16[4,1,88,3072]{3,2,1,0:T(8,128)(2,1)}, u32[]{:S(2)}, u32[]{:S(2)}) collective-permute-start(bf16[4,1,88,3072]{3,2,1,0:T(8,128)(2,1)} %shard_map.493.refs_0_), channel_id=1, source_target_pairs={{0,4},{2,6},{4,0},{6,2},{1,5},{3,7},{5,1},{7,3},{8,12},{10,14},{12... | collective-permute-start | bytes 6488072 | tf_op jit(solution)/shard_map/ppermute | solution.py:485
  521.5 602.7 %reduce-scatter.15.cloned.1.call-start = ((), (), s32[]{:S(2)}) async-start(), calls=%async_computation.13 | async-start | bytes 2703360 | tf_op jit(solution)/shard_map/reduce_scatter | solution.py:874
  821.9 113.8 %collective-permute-start.69 = (bf16[1,352,3072]{2,1,0:T(8,128)(2,1)}, bf16[1,352,3072]{2,1,0:T(8,128)(2,1)}, u32[]{:S(2)}, u32[]{:S(2)}) collective-permute-start(bf16[1,352,3072]{2,1,0:T(8,128)(2,1)} %get-tuple-element.488), channel_id=1, source_target_pairs={{0,4},{2,6},{4,0},{6,2},{1,5},{3,7},{5,1},{7,3},{8,12},{10,14},{12... | collective-permute-start | bytes 6488072 | tf_op jit(solution)/shard_map/ppermute | solution.py:485
  837.8 104.6 %collective-permute-start.74 = (bf16[1,352,3072]{2,1,0:T(8,128)(2,1)}, bf16[1,352,3072]{2,1,0:T(8,128)(2,1)}, u32[]{:S(2)}, u32[]{:S(2)}) collective-permute-start(bf16[1,352,3072]{2,1,0:T(8,128)(2,1)} %get-tuple-element.500), channel_id=1, source_target_pairs={{0,4},{2,6},{4,0},{6,2},{1,5},{3,7},{5,1},{7,3},{8,12},{10,14},{12... | collective-permute-start | bytes 6488072 | tf_op jit(solution)/shard_map/ppermute | solution.py:485
  946.8 177.4 %reduce-scatter.13.cloned.1.call-start = ((), (), s32[]{:S(2)}) async-start(), calls=%async_computation.12 | async-start | bytes 2703360 | tf_op jit(solution)/shard_map/reduce_scatter | solution.py:874
  947.5 335.7 %reduce-scatter.17.cloned.1.call-start = ((), (), s32[]{:S(2)}) async-start(), calls=%async_computation.14 | async-start | bytes 1351680 | tf_op jit(solution)/shard_map/reduce_scatter | solution.py:874
  1029.7 114.7 %collective-permute-start.81 = (bf16[4,352,704]{2,1,0:T(8,128)(2,1)}, bf16[4,352,704]{2,1,0:T(8,128)(2,1)}, u32[]{:S(2)}, u32[]{:S(2)}) collective-permute-start(bf16[4,352,704]{2,1,0:T(8,128)(2,1)} %get-tuple-element.531), channel_id=1, source_target_pairs={{0,4},{2,6},{4,0},{6,2},{1,5},{3,7},{5,1},{7,3},{8,12},{10,14},{12... | collective-permute-start | bytes 5947400 | tf_op jit(solution)/shard_map/ppermute | solution.py:485
  1077.4 205.9 %reduce-scatter.19.cloned.1.call-start = ((), (), s32[]{:S(2)}) async-start(), calls=%async_computation.15 | async-start | bytes 2703360 | tf_op jit(solution)/shard_map/reduce_scatter | solution.py:874
  1149.7 555.4 %reduce-scatter.35.cloned.1.call-start = ((), (), s32[]{:S(2)}) async-start(), calls=%async_computation.23 | async-start | bytes 2703360 | tf_op jit(solution)/shard_map/reduce_scatter | solution.py:874
  1151.4 153.7 %collective-permute-start.90 = (bf16[1,352,3072]{2,1,0:T(8,128)(2,1)}, bf16[1,352,3072]{2,1,0:T(8,128)(2,1)}, u32[]{:S(2)}, u32[]{:S(2)}) collective-permute-start(bf16[1,352,3072]{2,1,0:T(8,128)(2,1)} %get-tuple-element.575), channel_id=1, source_target_pairs={{0,4},{2,6},{4,0},{6,2},{1,5},{3,7},{5,1},{7,3},{8,12},{10,14},{12... | collective-permute-start | bytes 6488072 | tf_op jit(solution)/shard_map/ppermute | solution.py:485
  1309.3 402.0 %reduce-scatter.27.cloned.1.call-start = ((), (), s32[]{:S(2)}) async-start(), calls=%async_computation.19 | async-start | bytes 1351680 | tf_op jit(solution)/shard_map/reduce_scatter | solution.py:874
  1487.9 224.4 %reduce-scatter.31.cloned.1.call-start = ((), (), s32[]{:S(2)}) async-start(), calls=%async_computation.21 | async-start | bytes 983040 | tf_op jit(solution)/shard_map/reduce_scatter | solution.py:874
  1494.3 218.1 %reduce-scatter.29.cloned.1.call-start = ((), (), s32[]{:S(2)}) async-start(), calls=%async_computation.20 | async-start | bytes 983040 | tf_op jit(solution)/shard_map/reduce_scatter | solution.py:874
  1559.3 159.4 %reduce-scatter.33.cloned.1.call-start = ((), (), s32[]{:S(2)}) async-start(), calls=%async_computation.22 | async-start | bytes 2703360 | tf_op jit(solution)/shard_map/reduce_scatter | solution.py:874
  1566.8 158.0 %reduce-scatter.23.cloned.1.call-start = ((), (), s32[]{:S(2)}) async-start(), calls=%async_computation.17 | async-start | bytes 1351680 | tf_op jit(solution)/shard_map/reduce_scatter | solution.py:874
  1594.0 130.8 %reduce-scatter.21.cloned.1.call-start = ((), (), s32[]{:S(2)}) async-start(), calls=%async_computation.16 | async-start | bytes 1351680 | tf_op jit(solution)/shard_map/reduce_scatter | solution.py:874
  (577 other events, 8306.6 us)
Sparse Core Ops, SparseCore 0:
  32.9 57.8 all-gather.14
  93.0 47.4 all-gather.16
  142.6 44.9 all-gather.18
  189.6 45.9 all-gather.20
  237.6 45.9 all-gather.22
  331.8 49.7 all-gather.24
  521.6 47.9 all-gather.26
  946.9 45.7 reduce-scatter.14
  995.7 44.3 reduce-scatter.12
  1077.5 28.4 reduce-scatter.16
  1149.8 46.0 reduce-scatter.18
  1309.5 46.0 reduce-scatter.34
  1488.1 28.9 reduce-scatter.26
  1519.8 21.9 reduce-scatter.30
  1559.4 24.4 reduce-scatter.28
  1586.7 46.3 reduce-scatter.32
  1635.8 27.0 reduce-scatter.22
  1681.5 25.9 reduce-scatter.20
  1710.5 43.6 reduce-scatter.24
where the time goes:
time: 1780 us
  Pallas kernels  677 us (38%)
  waiting for transfers between devices  551 us (31%)
  local copies, waits for them, and re-layouts  224 us (13%)
  starting transfers between devices  169 us (9%)
  other arithmetic  127 us (7%)
  between operations  19.6 us (1%)
    ppermute x69, waiting for transfers between devices, swap_context(): return lax.ppermute(in_rows(operand), CONTEXT, pairs).reshape(operand.shape)  351 us
    pallas_call x12, Pallas kernels, grad_core(): pl.pallas_call(lambda *refs: grad_kernel(which, spread, tile, counts, len...  200 us
    unnamed x905, local copies, waits for them, and re-layouts  195 us
    pallas_call x32, Pallas kernels, multiply(): pl.pallas_call(kernel, grid=(pl.cdiv(width, tile),), in_specs=[pl.BlockSp...  162 us
    ppermute x44, waiting for transfers between devices, swap_tensor(): lax.ppermute(in_rows(operand), TENSOR, [(0, 1), (1, 0)])  129 us
    pallas_call x11, Pallas kernels, share_core(): pl.pallas_call(lambda *refs: share_kernel(count, widths, *refs), in_specs...  108 us
    ppermute x27, starting transfers between devices, shift_fsdp(): lax.ppermute(operand, FSDP, [(i, (i + step) % size) for i in range(size)])  65.7 us
    ppermute x44, starting transfers between devices, swap_tensor(): lax.ppermute(in_rows(operand), TENSOR, [(0, 1), (1, 0)])  51.2 us
  transfers between devices with their start and end apart: 159, of which 54 were waited for; matrix products, arithmetic and copies ran while one was open for 9% of the time, Pallas kernels for 37%

commit v1 on v0

--- a/solution.py
+++ b/solution.py
@@ -41,7 +41,7 @@
 def gate(operand, after):
     return pl.pallas_call(
         lambda *refs: None,
-        in_specs=[IN_HBM] + [FREE] * len(after),
+        in_specs=[IN_HBM] + [IN_HBM] * len(after),
         out_specs=IN_HBM,
         out_shape=jax.ShapeDtypeStruct(operand.shape, operand.dtype),
         input_output_aliases={0: 0},
@@ -121,7 +121,7 @@
     return pl.pallas_call(
         turn_kernel,
         grid=(rows // min(rows, 128),),
-        in_specs=[spec] * 4 + [FREE] * len(after),
+        in_specs=[spec] * 4 + [IN_HBM] * len(after),
         out_specs=[spec, spec, TOKEN_SPEC],
         out_shape=[shape, shape, TOKEN],
         compiler_params=vmem(32),
@@ -144,7 +144,7 @@
     return pl.pallas_call(
         turn_back_kernel,
         grid=(rows // min(rows, 128),),
-        in_specs=[spec] * 4 + [FREE] * len(after),
+        in_specs=[spec] * 4 + [IN_HBM] * len(after),
         out_specs=[spec, TOKEN_SPEC],
         out_shape=[jax.ShapeDtypeStruct((rows, width), LOW), TOKEN],
         compiler_params=vmem(32),
@@ -165,7 +165,7 @@
     return pl.pallas_call(
         root_kernel,
         grid=(rows // min(rows, 128),),
-        in_specs=[spec] + [FREE] * len(after),
+        in_specs=[spec] + [IN_HBM] * len(after),
         out_specs=[spec, TOKEN_SPEC],
         out_shape=[jax.ShapeDtypeStruct((rows, width), LOW), TOKEN],
         compiler_params=vmem(32),
@@ -215,7 +215,7 @@
     return pl.pallas_call(
         lambda *refs: attend_kernel(count, *refs),
         grid=(seqs,),
-        in_specs=[block_of(query)] * (1 + 2 * count) + [FREE] * len(after),
+        in_specs=[block_of(query)] * (1 + 2 * count) + [IN_HBM] * len(after),
         out_specs=[
             block_of(query),
             pl.BlockSpec((1, heads, parts * tokens), lambda s: (s, 0, 0)),
@@ -292,7 +292,7 @@
             block_of(sin),
         ]
         + [spec] * (2 * count)
-        + [FREE] * len(after),
+        + [IN_HBM] * len(after),
         out_specs=[spec] * (1 + 2 * count) + [TOKEN_SPEC],
         out_shape=[shape] * (1 + 2 * count) + [TOKEN],
         compiler_params=vmem(56),
@@ -332,7 +332,7 @@
         lambda *refs: cross_kernel(count, *refs),
         grid=(seqs,),
         in_specs=[sequence_block(operand) for operand in (query_raw, key, value)]
-        + [FREE] * len(after),
+        + [IN_HBM] * len(after),
         out_specs=[sequence_block(query_raw), TOKEN_SPEC],
         out_shape=[jax.ShapeDtypeStruct(query_raw.shape, LOW), TOKEN],
         compiler_params=vmem(32),
@@ -371,7 +371,7 @@
         lambda *refs: cross_back_kernel(count, *refs),
         grid=(seqs,),
         in_specs=[sequence_block(operand) for operand in (query_raw, key_raw, key, value, grad)]
-        + [FREE] * len(after),
+        + [IN_HBM] * len(after),
         out_specs=[sequence_block(operand) for operand in (query_raw, key_raw, value)]
         + [TOKEN_SPEC],
         out_shape=[
@@ -425,7 +425,7 @@
     return pl.pallas_call(
         lambda *refs: add_kernel(len(pairs), cut, *refs),
         grid=(count,),
-        in_specs=[spec] * len(operands) + [FREE] * len(after),
+        in_specs=[spec] * len(operands) + [IN_HBM] * len(after),
         out_specs=[out_spec] * len(pairs) + [TOKEN_SPEC],
         out_shape=[shape] * len(pairs) + [TOKEN],
         compiler_params=vmem(40),
@@ -606,7 +606,7 @@
         in_specs=[pl.BlockSpec(left.shape, lambda j: (0, 0)) for left in lefts]
         + [right_block(right) for right in rights]
         + [column_block(extra.shape[0]) for extra in extras]
-        + [FREE] * len(after),
+        + [IN_HBM] * len(after),
         out_specs=[column_block(rows) for rows, _, _ in outs] + [TOKEN_SPEC],
         out_shape=[jax.ShapeDtypeStruct((rows, wide_by), kind) for rows, wide_by, kind in outs]
         + [TOKEN],
@@ -647,9 +647,87 @@
     return other
 
 
-def share_kernel(count, widths, *refs):
-    sources, outs = refs[:count], refs[-count // 2 * widths - 4 :]
-    targets, token_ref = outs[: count // 2 * widths], outs[-4]
+FAR = "far"
+
+
+def partner(kind):
+    if isinstance(kind, list):
+        return {**partner(kind[0]), **partner(kind[1])}
+    return partner_on_axis(kind)
+
+
+def partner_on_axis(kind):
+    place = lax.axis_index(CONTEXT)
+    if kind == TENSOR:
+        return {TENSOR: 1 - lax.axis_index(TENSOR)}
+    if kind == CORE:
+        return {CONTEXT: place + 1 - 2 * (place % 2)}
+    if kind == CHIP:
+        return {CONTEXT: (place + CHIP) % 4}
+    if kind == FAR:
+        return {CONTEXT: (place + CHIP + 1 - 2 * (place % 2)) % 4}
+    size = lax.axis_size(FSDP)
+    return {FSDP: (lax.axis_index(FSDP) + kind[0]) % size}
+
+
+def meet(kinds):
+    barrier = pltpu.get_barrier_semaphore()
+    for kind in kinds:
+        pl.semaphore_signal(barrier, inc=1, device_id=partner(kind), device_id_type=MESH)
+    pl.semaphore_wait(barrier, len(kinds))
+
+
+def sending(source, target, sems, index, kind):
+    return pltpu.make_async_remote_copy(
+        src_ref=source,
+        dst_ref=target,
+        send_sem=sems.at[0, index],
+        recv_sem=sems.at[1, index],
+        device_id=partner(kind),
+        device_id_type=MESH,
+    )
+
+
+def distinct(kinds):
+    return [kind for index, kind in enumerate(kinds) if kind not in kinds[:index]]
+
+
+def exchange_kernel(kinds, *refs):
+    count = len(kinds)
+    sources, targets, token_ref, sems = refs[:count], refs[-count - 2 : -2], refs[-2], refs[-1]
+    mark(token_ref)
+    meet(distinct(kinds))
+    copies = [
+        sending(source, target, sems, index, kind)
+        for index, (source, target, kind) in enumerate(zip(sources, targets, kinds))
+    ]
+    for copy in copies:
+        copy.start()
+    for copy in copies:
+        copy.wait()
+
+
+def exchange(items, after, ident):
+    operands, kinds = zip(*items)
+    return pl.pallas_call(
+        lambda *refs: exchange_kernel(list(kinds), *refs),
+        in_specs=[FREE] * len(items) + [IN_HBM] * len(after),
+        out_specs=[FREE] * len(items) + [WHOLE],
+        out_shape=[jax.ShapeDtypeStruct(operand.shape, operand.dtype) for operand in operands]
+        + [TOKEN],
+        scratch_shapes=[pltpu.SemaphoreType.DMA((2, len(items)))],
+        compiler_params=pltpu.CompilerParams(
+            collective_id=ident, has_side_effects=True, vmem_limit_bytes=16 * MIB
+        ),
+        cost_estimate=cost(0, 0),
+    )(*operands, *after)
+
+
+def share_kernel(count, places, *refs):
+    widths = len(places)
+    total = 1 + places[-1][0]
+    sources, outs = refs[:count], refs[-count // 2 * total - 4 :]
+    targets, token_ref = outs[:-4], outs[-4]
     local_sem, send_sem, recv_sem = outs[-3:]
     mark(token_ref)
     place = lax.axis_index(CONTEXT)
@@ -661,7 +739,9 @@
         for index in range(widths):
             sem = source_at * widths + index
             source = sources[source_at].at[:, index]
-            target = targets[part * widths + index].at[:, slot]
+            out_at, half = places[index]
+            target = targets[part * total + out_at]
+            target = target.at[:, slot] if half is None else target.at[:, slot, half]
             remote = pltpu.make_async_remote_copy(
                 src_ref=source,
                 dst_ref=target,
@@ -678,25 +758,30 @@
         copy.wait()
 
 
-def share_core(pieces, after, ident):
+def share_core(pieces, after, ident, halved=False):
     along, widths, rows, width = pieces[0].shape
     count = len(pieces)
     size = lax.axis_size(CONTEXT)
-    total = count // 2 * widths
-    shape = jax.ShapeDtypeStruct((along, size, rows, width), LOW)
+    places = [(index, None) for index in range(widths)]
+    shapes = [(along, size, rows, width)] * widths
+    if halved:
+        places = [(0, 0), (0, 1)] + [(index, None) for index in range(1, widths - 1)]
+        shapes = [(along, size, 2, rows, width)] + shapes[2:]
+    total = count // 2 * len(shapes)
     outs = pl.pallas_call(
-        lambda *refs: share_kernel(count, widths, *refs),
-        in_specs=[WHOLE] * count + [FREE] * len(after),
+        lambda *refs: share_kernel(count, places, *refs),
+        in_specs=[WHOLE] * count + [IN_HBM] * len(after),
         out_specs=[IN_HBM] * total + [WHOLE],
-        out_shape=[shape] * total + [TOKEN],
+        out_shape=[jax.ShapeDtypeStruct(shape, LOW) for shape in shapes] * (count // 2) + [TOKEN],
         scratch_shapes=[pltpu.SemaphoreType.DMA((count * widths,))] * 3,
         compiler_params=pltpu.CompilerParams(
             collective_id=ident, has_side_effects=True, vmem_limit_bytes=40 * MIB
         ),
         cost_estimate=cost(0, 6 * count * pieces[0].size * 2),
     )(*pieces, *after)
-    held = [out.reshape(along * size * rows, width) for out in outs[:-1]]
-    return [held[part * widths : (part + 1) * widths] for part in range(count // 2)], outs[-1]
+    held = [out.reshape(-1, width) for out in outs[:-1]]
+    each = len(shapes)
+    return [held[part * each : (part + 1) * each] for part in range(count // 2)], outs[-1]
 
 
 def pack_of(shards):
@@ -838,7 +923,7 @@
     shape = jax.ShapeDtypeStruct((jobs // count, rows, width), LOW)
     outs = pl.pallas_call(
         lambda *refs: grad_kernel(which, spread, tile, counts, len(after), *refs),
-        in_specs=[WHOLE] * (len(lefts) + jobs) + [FREE] * len(after),
+        in_specs=[WHOLE] * (len(lefts) + jobs) + [IN_HBM] * len(after),
         out_specs=[WHOLE] * (2 * count + 1),
         out_shape=[shape] * (2 * count) + [TOKEN],
         scratch_shapes=[
@@ -1015,7 +1100,16 @@
     return after_cross + gate_m * kept.mlp_branch, kept
 
 
-def layer_backward(grad_res, kept, weights, modulation, tables, text, text_low, order, earlier):
+def modulate(columns):
+    if paired():
+        total = columns[0] + swap_tensor(columns[1])
+    else:
+        total = lax.psum_scatter(jnp.stack(columns), TENSOR, scatter_dimension=0, tiled=False)
+    mod_all = gather_fsdp_small(sum_context(total))
+    return mod_all.reshape(-1, mod_all.shape[-1])
+
+
+def layer_backward(grad_res, kept, weights, modulation, tables, text, text_low, order, earlier, last):
     rows, features = grad_res.shape
     parts = lax.axis_size(TENSOR)
     every = rows * parts
@@ -1158,10 +1252,8 @@
         [(text_low.shape[0], text_low.shape[1], jnp.float32)],
         256,
     )
-    crossed = sum_parts(*crossed, order)
     earlier.third()
     key_grad, value_grad = order.put(add_pairs(whole, 0, order.after))
-    crossed = (crossed[0], swap_context(gate(crossed[1], order.after), CHIP))
     (key_grad,) = order.put(turn_back(key_grad[0], kept.key_raw, cos, sin, order.after))
     value_grad = value_grad[0]
     terms = order.multiply(
@@ -1175,12 +1267,20 @@
         term_shapes(every, features),
     )
     attn_in_grad = sum_tensor(terms)
-    attended = product(
-        [attn_grad, kept.attn_all],
-        [kept.attn_low, query_grad, key_grad, value_grad],
-        (0, 1, 1, 1),
-        0,
-    )
+    order.need(*earlier.most())
+    attn_own, attn_given = order.put(
+        grad_core(
+            [attn_grad, kept.attn_all],
+            [kept.attn_low, query_grad, key_grad, value_grad],
+            (0, 1, 1, 1),
+            0,
+            order.after,
+            order.ident(),
+        )
+    )
+    attended = (attn_own,) if last else (attn_own, swap_context(attn_given, CHIP))
+    crossed = sum_parts(*crossed, order)
+    crossed = (crossed[0], swap_context(crossed[1], CHIP))
     texts = sum_parts(*texts, order)
     texts = (texts[0], swap_context(texts[1], CHIP))
     grad_shift_a = per_sequence(attn_in_grad, seqs)
@@ -1198,6 +1298,9 @@
         [],
         [(rows, 2 * features, jnp.float32)],
     )
+    mod_grad = jnp.concatenate(
+        [grad_shift_a, grad_scale_a, grad_gate_a, grad_shift_m, grad_scale_m, grad_gate_m], axis=-1
+    )
     later = SimpleNamespace()
 
     def start():
@@ -1215,23 +1318,62 @@
     def third():
         reduced.skip = sum_rest(*later.skipped, order)
 
+    def end(text_total):
+        if not last:
+            start()
+            first()
+            second()
+            third()
+            return modulate(columns_of(mod_grad)), sum_text(text_total)
+        order.need(reduced.up)
+        (own, other), (chip_own, chip_other) = product(
+            [[kept.concat_low]], skip_grad, (0,) * parts, parts
+        )
+        order.need(*earlier.rest())
+        reduced.cross = sum_rest(*crossed, order)
+        reduced.text = sum_rest(*texts, order)
+        columns = columns_of(mod_grad)
+        came = order.put(
+            exchange(
+                [
+                    (other, TENSOR),
+                    (chip_other, TENSOR),
+                    (attn_given, CHIP),
+                    (columns[1], TENSOR),
+                ],
+                order.after,
+                order.ident(),
+            )
+        )
+        columns_came = came[3]
+        order.need(reduced.cross, reduced.text)
+        reduced.attention = sum_rest(attended[0], came[2], order)
+        own, chip_own = order.put(
+            add_pairs([(own, came[0]), (chip_own, came[1])], 0, order.after)
+        )
+        total = columns[0] + columns_came
+        chip_came, *totals = order.put(
+            exchange(
+                [(chip_own, CHIP), (total, CHIP), (total, CORE), (total, FAR)],
+                order.after,
+                order.ident(),
+            )
+        )
+        text_total = gate(text_total, order.after)
+        order.need(reduced.attention)
+        reduced.skip = sum_rest(own, chip_came, order)
+        mod_all = gather_fsdp_small(total + totals[0] + totals[1] + totals[2])
+        return mod_all.reshape(-1, mod_all.shape[-1]), sum_text(text_total)
+
     later.start, later.first, later.second, later.third = start, first, second, third
+    later.end = end
     concat_grad = layer_norm_back(kept.concat, concat_grad)
-    mod_grad = jnp.concatenate(
-        [grad_shift_a, grad_scale_a, grad_gate_a, grad_shift_m, grad_scale_m, grad_gate_m], axis=-1
-    )
-    mod_columns = columns_of(mod_grad)
-    if paired():
-        mod_columns = mod_columns[0] + swap_tensor(mod_columns[1])
-    else:
-        mod_columns = lax.psum_scatter(
-            jnp.stack(mod_columns), TENSOR, scatter_dimension=0, tiled=False
-        )
-    mod_all = gather_fsdp_small(sum_context(mod_columns))
-    mod_all = mod_all.reshape(-1, mod_all.shape[-1])
+    later.columns = lambda: modulate(columns_of(mod_grad))
     later.sums = lambda: (reduced.down, reduced.up)
     later.more = lambda: (reduced.cross, reduced.attention)
-    return concat_grad[:, :features], concat_grad[:, features:], mod_all, text_part, reduced, later
+    later.most = lambda: (reduced.text,)
+    later.rest = lambda: (reduced.skip,)
+    return concat_grad[:, :features], concat_grad[:, features:], text_part, reduced, later
 
 
 def shards(
@@ -1264,6 +1406,10 @@
     def cross_of(layer):
         return [proj_weight[layer, :, 3], output_weight[layer, 1].T]
 
+    def halves_of(shard):
+        half = shard.shape[0] // 2
+        return [shard[:half], shard[half:]]
+
     def attention_of(layer):
         return [proj_weight[layer, :, j] for j in range(3)] + [output_weight[layer, 0].T]
 
@@ -1273,17 +1419,18 @@
     arrived = (skip_along,)
     skip_parts = across(skip_along, True, ())
     started = (skip_parts[1],)
-    cross_along = [gather_fsdp_small(gate(pack_of(cross_of(0)), arrived))]
-    skips = [skip_along]
-    for layer in every[1:]:
-        skips.append(gather_fsdp_small(gate(pack_of([skip_weight[layer]]), started)))
-        cross_along.append(gather_fsdp_small(gate(pack_of(cross_of(layer)), started)))
-    attention = [gather_fsdp(attention_of(0), arrived)]
+    mixed = gather_fsdp(attention_of(0) + cross_of(0), arrived)
+    attention, crosses, skips = [mixed[:, :4]], [mixed[:, 4:]], [None]
     text_along = gather_fsdp([text_weight[i, :, j] for i in every for j in range(2)], arrived)
     ups = [gather_fsdp([up_weight[0]], arrived)]
     downs = [gather_fsdp([down_weight[0].T], arrived)]
     for layer in every[1:]:
-        attention.append(gather_fsdp(attention_of(layer), started))
+        mixed = gather_fsdp(
+            attention_of(layer) + cross_of(layer) + halves_of(skip_weight[layer]), started
+        )
+        attention.append(mixed[:, :4])
+        crosses.append(mixed[:, 4:6])
+        skips.append(mixed[:, 6:])
         ups.append(gather_fsdp([up_weight[layer]], started))
         downs.append(gather_fsdp([down_weight[layer].T], started))
 
@@ -1291,7 +1438,9 @@
     skip_parts = {0: skip_parts}
 
     def hold_skip(layer):
-        (held,) = order.put(share_core(skip_parts[layer], order.after, order.ident()))
+        (held,) = order.put(
+            share_core(skip_parts[layer], order.after, order.ident(), layer > 0)
+        )
         weights[layer].skip = [part[0] for part in held]
 
     def hold_attention(layer):
@@ -1344,7 +1493,6 @@
 
     text_parts = {}
     attention_parts[0] = across(attention[0], False, (skip_parts[0][-1],))
-    order.need(cross_along[0])
     hold_skip(0)
 
     def steps_of(layer):
@@ -1359,35 +1507,35 @@
         def turned():
             if layer:
                 read_text(layer)
-            else:
-                cross_parts[layer] = across(cross_along[layer], True, order.after)
 
         def attended():
             if layer:
                 down_parts[layer] = across(downs[layer], False, order.after)
                 hold_up(layer)
             else:
+                cross_parts[layer] = across(crosses[layer], True, order.after)
                 up_parts[layer] = across(ups[layer], False, order.after)
                 hold_text()
-                down_parts[layer] = across(downs[layer], False, order.after)
+                if coming:
+                    skip_parts[coming] = across(skips[coming], True, order.after)
                 read_text(layer)
                 if coming:
-                    order.need(skips[coming])
+                    order.need(skip_parts[coming][1])
             hold_cross(layer)
-            if coming:
-                skip_parts[coming] = across(skips[coming], True, order.after)
+            if not layer:
+                down_parts[layer] = across(downs[layer], False, order.after)
 
         def crossed():
             if not layer:
                 hold_up(layer)
             if coming:
                 attention_parts[coming] = across(attention[coming], False, order.after)
-                order.need(cross_along[coming])
 
         def raised():
             hold_down(layer)
             if coming:
-                cross_parts[coming] = across(cross_along[coming], True, order.after)
+                order.need(attention_parts[coming][1])
+                cross_parts[coming] = across(crosses[coming], True, order.after[:1])
 
         def lowered():
             if coming:
@@ -1456,15 +1604,24 @@
     block_output = low(residual).reshape(latents.shape)
 
     grad_res = wide(cotangent).reshape(own)
-    cond_total = 0.0
+    cond_parts = []
     text_total = 0.0
     skip_grads = [None] * layers
     gradients = [None] * layers
+
+    def add_modulation(layer, mod_all):
+        gradients[layer].mod = jnp.einsum(
+            "bk,bc->kc", wide(cond_rows), mod_all, precision=PRECISE
+        )
+        cond_parts.append(
+            jnp.einsum("bc,kc->bk", mod_all, wide(mod_low[layer]), precision=PRECISE)
+        )
+
     later = SimpleNamespace(
-        start=lambda: None, first=lambda: None, second=lambda: None, third=lambda: None, sums=lambda: (), more=lambda: ()
+        start=lambda: None, first=lambda: None, second=lambda: None, third=lambda: None, sums=lambda: (), more=lambda: (), most=lambda: ()
     )
     for layer in reversed(every):
-        grad_res, skip_grads[layer], mod_all, text_part, reduced, later = layer_backward(
+        grad_res, skip_grads[layer], text_part, reduced, later = layer_backward(
             grad_res,
             stored[layer],
             weights[layer],
@@ -1474,17 +1631,14 @@
             text_low,
             order,
             later,
-        )
-        reduced.mod = jnp.einsum("bk,bc->kc", wide(cond_rows), mod_all, precision=PRECISE)
-        cond_total = cond_total + jnp.einsum(
-            "bc,kc->bk", mod_all, wide(mod_low[layer]), precision=PRECISE
+            paired() and layer == 0,
         )
         text_total = text_total + text_part
         gradients[layer] = reduced
-    later.start()
-    later.first()
-    later.second()
-    later.third()
+        if layer:
+            add_modulation(layer, later.columns())
+    mod_all, text_sum = later.end(low(text_total))
+    add_modulation(0, mod_all)
     gradients = [
         (
             wide(each.skip[0]),
@@ -1497,8 +1651,8 @@
         )
         for each in gradients
     ]
-    text_sum = sum_text(low(text_total))
     text_sum = wide(text_sum).reshape(seqs, padded, -1)[:, :text_count]
+    cond_total = sum(cond_parts)
     if paired():
         cond_total = cond_total + swap_tensor(cond_total)
     else:

time: 1780 us -> 1690 us (0.949)
  waiting for transfers between devices: 551 us -> 431 us
  Pallas kernels: 677 us -> 755 us
  starting transfers between devices: 169 us -> 130 us
    ppermute x69 -> x65, waiting for transfers between devices: 351 us -> 235 us  [swap_context(): return lax.ppermute(in_rows(operand), CONTEXT, pairs).reshape(operand.shape)]
    pallas_call x40 -> x38, Pallas kernels: 108 us -> 195 us  [the longest x11 106 us: share_core(): pl.pallas_call(lambda *refs: share_kernel(count, places, *refs), in_specs...]
    ppermute x44 -> x41, waiting for transfers between devices: 129 us -> 173 us  [swap_tensor(): lax.ppermute(in_rows(operand), TENSOR, [(0, 1), (1, 0)])]
    ppermute x27 -> x18, waiting for transfers between devices: 44.1 us -> 10.3 us  [shift_fsdp(): lax.ppermute(operand, FSDP, [(i, (i + step) % size) for i in range(size)])]
    ppermute x27 -> x18, starting transfers between devices: 65.7 us -> 32.2 us  [shift_fsdp(): lax.ppermute(operand, FSDP, [(i, (i + step) % size) for i in range(size)])]
    ppermute x44 -> x41, starting transfers between devices: 51.2 us -> 48.3 us  [swap_tensor(): lax.ppermute(in_rows(operand), TENSOR, [(0, 1), (1, 0)])]
    unnamed x905 -> x920, local copies, waits for them, and re-layouts: 195 us -> 192 us
    ppermute x69 -> x65, starting transfers between devices: 49.5 us -> 48.4 us  [swap_context(): return lax.ppermute(in_rows(operand), CONTEXT, pairs).reshape(operand.shape)]
  transfers between devices with their start and end apart: 159 -> 143, of which waited for: 54 -> 48; matrix products, arithmetic and copies ran while one was open for 9% -> 10% of each run, Pallas kernels for 37% -> 42%
where the time goes in v1:
time: 1690 us; the launch traced here: 1670 us
  Pallas kernels  755 us (45%)
  waiting for transfers between devices  431 us (26%)
  local copies, waits for them, and re-layouts  217 us (13%)
  starting transfers between devices  130 us (8%)
  other arithmetic  113 us (7%)
  between operations  19.8 us (1%)
    ppermute x65, waiting for transfers between devices, swap_context(): return lax.ppermute(in_rows(operand), CONTEXT, pairs).reshape(operand.shape)  235 us
    unnamed x920, local copies, waits for them, and re-layouts  192 us
    pallas_call x12, Pallas kernels, grad_core(): pl.pallas_call(lambda *refs: grad_kernel(which, spread, tile, counts, len...  183 us
    ppermute x41, waiting for transfers between devices, swap_tensor(): lax.ppermute(in_rows(operand), TENSOR, [(0, 1), (1, 0)])  173 us
    pallas_call x32, Pallas kernels, multiply(): pl.pallas_call(kernel, grid=(pl.cdiv(width, tile),), in_specs=[pl.BlockSp...  171 us
    pallas_call x11, Pallas kernels, share_core(): pl.pallas_call(lambda *refs: share_kernel(count, places, *refs), in_specs...  106 us
    pallas_call x2, Pallas kernels, exchange(): pl.pallas_call(lambda *refs: exchange_kernel(list(kinds), *refs), in_spec...  89.3 us
    ppermute x65, starting transfers between devices, swap_context(): return lax.ppermute(in_rows(operand), CONTEXT, pairs).reshape(operand.shape)  48.4 us
  transfers between devices with their start and end apart: 143, of which 48 were waited for; matrix products, arithmetic and copies ran while one was open for 10% of the time, Pallas kernels for 42%

profile of v1, /device:TPU:0, one launch (start us, length us, event | category | flops | bytes accessed | tf_op | source)
XLA Modules:
  0.0 1673.5 jit_solution(11374399181225246843)
XLA Ops:
  72.7 15.0 collective-permute-done.3.refs_0_
  93.3 21.1 %collective-permute-done.5.refs_3_.refs_1_ = bf16[4,1,176,704]{3,2,1,0:T(8,128)(2,1)S(1)} collective-permute-done((bf16[4,1,176,704]{3,2,1,0:T(8,128)(2,1)}, bf16[4,1,176,704]{3,2,1,0:T(8,128)(2,1)S(1)}, u32[]{:S(2)}, u32[]{:S(2)}) %collective-permute-start.5) | collective-permute-done | bytes 991264 | tf_op jit(solution)/shard_map/ppermute | solution.py:489
  153.3 39.5 %collective-permute-done.16.refs_1_ = bf16[4,4,88,704]{3,2,1,0:T(8,128)(2,1)} collective-permute-done((bf16[4,4,88,704]{3,2,1,0:T(8,128)(2,1)}, bf16[4,4,88,704]{3,2,1,0:T(8,128)(2,1)}, u32[]{:S(2)}, u32[]{:S(2)}) %collective-permute-start.16) | collective-permute-done | bytes 1982496 | tf_op jit(solution)/shard_map/ppermute | solution.py:485
  226.5 16.8 %collective-permute-done.17 = bf16[64,8,704]{2,1,0:T(8,128)(2,1)} collective-permute-done((bf16[64,8,704]{2,1,0:T(8,128)(2,1)}, bf16[64,8,704]{2,1,0:T(8,128)(2,1)}, u32[]{:S(2)}, u32[]{:S(2)}) %collective-permute-start.17) | collective-permute-done | bytes 720928 | tf_op jit(solution)/shard_map/ppermute | solution.py:485
  334.0 15.4 shard_map.477
  358.9 17.0 %collective-permute-done.30.refs_0_ = bf16[4,2,88,704]{3,2,1,0:T(8,128)(2,1)} collective-permute-done((bf16[4,2,88,704]{3,2,1,0:T(8,128)(2,1)}, bf16[4,2,88,704]{3,2,1,0:T(8,128)(2,1)}, u32[]{:S(2)}, u32[]{:S(2)}) %collective-permute-start.30) | collective-permute-done | bytes 991264 | tf_op jit(solution)/shard_map/ppermute | solution.py:485
  433.0 17.0 %collective-permute-done.32.refs_1_ = bf16[256,1408]{1,0:T(8,128)(2,1)S(1)} collective-permute-done((bf16[256,1408]{1,0:T(8,128)(2,1)S(1)}, bf16[256,1408]{1,0:T(8,128)(2,1)S(1)}, u32[]{:S(2)}, u32[]{:S(2)}) %collective-permute-start.32) | collective-permute-done | bytes 720928 | tf_op jit(solution)/shard_map/ppermute | solution.py:489
  475.6 17.9 %collective-permute-done.35.refs_3_.refs_1_ = bf16[4,4,88,704]{3,2,1,0:T(8,128)(2,1)} collective-permute-done((bf16[4,4,88,704]{3,2,1,0:T(8,128)(2,1)}, bf16[4,4,88,704]{3,2,1,0:T(8,128)(2,1)}, u32[]{:S(2)}, u32[]{:S(2)}) %collective-permute-start.35) | collective-permute-done | bytes 1982496 | tf_op jit(solution)/shard_map/ppermute | solution.py:485
  584.4 16.8 %collective-permute-done.42 = bf16[64,8,704]{2,1,0:T(8,128)(2,1)} collective-permute-done((bf16[64,8,704]{2,1,0:T(8,128)(2,1)}, bf16[64,8,704]{2,1,0:T(8,128)(2,1)}, u32[]{:S(2)}, u32[]{:S(2)}) %collective-permute-start.42) | collective-permute-done | bytes 720928 | tf_op jit(solution)/shard_map/ppermute | solution.py:485
  691.0 16.3 collective-permute-done.50.refs_1_
  855.7 14.8 shard_map.531
  875.0 21.9 %shard_map.533 = (bf16[2,2,128,704]{3,2,1,0:T(8,128)(2,1)}, bf16[2,2,128,704]{3,2,1,0:T(8,128)(2,1)}, bf16[2,2,128,704]{3,2,1,0:T(8,128)(2,1)}, bf16[2,2,128,704...) custom-call(bf16[2,2,128,704]{3,2,1,0:T(8,128)(2,1)} %bitcast.716, ...), custom_call_target="tpu_custom_call" | custom-call | flops 10737418 | bytes 14417 | tf_op jit(solution)/shard_map/pallas_call | solution.py:283
  959.2 15.1 shard_map.541
  979.6 16.2 collective-permute-done.66
  1043.1 17.4 %collective-permute-done.69.refs_1_ = bf16[256,1408]{1,0:T(8,128)(2,1)S(1)} collective-permute-done((bf16[256,1408]{1,0:T(8,128)(2,1)S(1)}, bf16[256,1408]{1,0:T(8,128)(2,1)S(1)}, u32[]{:S(2)}, u32[]{:S(2)}) %collective-permute-start.69) | collective-permute-done | bytes 720928 | tf_op jit(solution)/shard_map/ppermute | solution.py:489
  1086.1 15.1 shard_map.549
  1126.3 14.9 shard_map.551
  1189.3 15.7 shard_map.558
  1205.1 20.6 %shard_map.559 = (bf16[2,256,704]{2,1,0:T(8,128)(2,1)}, bf16[2,256,704]{2,1,0:T(8,128)(2,1)}, bf16[2,256,704]{2,1,0:T(8,128)(2,1)}, bf16[2,256,704]{2,1,0:T(8,128)(2,1)}, f32[8,128]{1,0:T(8,128)}) custom-call(bf16[768,1024]{1,0:T(8,128)(2,1)} %bitcast.599, bf16[768,704]{1,0:T(8,128)(2,1)} %bitcast.684, bf16[768,704]{1,0:T(8,128)(2,1)} %bitcast.688, ...), custom_call_target="tpu_custom_call" | custom-call | flops 4429185 | bytes 4325 | tf_op jit(solution)/shard_map/pallas_call | solution.py:924
  1230.4 21.9 %shard_map.561 = (bf16[2,2,128,704]{3,2,1,0:T(8,128)(2,1)}, bf16[2,2,128,704]{3,2,1,0:T(8,128)(2,1)}, bf16[2,2,128,704]{3,2,1,0:T(8,128)(2,1)}, bf16[2,2,128,704...) custom-call(bf16[2,2,128,704]{3,2,1,0:T(8,128)(2,1)} %bitcast.731, ...), custom_call_target="tpu_custom_call" | custom-call | flops 10737418 | bytes 14417 | tf_op jit(solution)/shard_map/pallas_call | solution.py:283
  1365.3 16.6 shard_map.570
  1428.8 15.2 shard_map.574
  1461.8 57.2 %shard_map.577 = (bf16[1,704,704]{2,1,0:T(8,128)(2,1)S(1)}, bf16[1,704,704]{2,1,0:T(8,128)(2,1)S(1)}, bf16[4,352,704]{2,1,0:T(8,128)(2,1)S(1)}, f32[2,4224]{1,0:T(2,128)S(1)}, f32[8,128]{1,0:T(8,128)S(1)}) custom-call(bf16[1,704,704]{2,1,0:T(8,128)(2,1)S(1)} %copy-done.272, bf16[1,704,704]{2,1,0:T(8,128)(2,1)S(1)} %copy-done.273, ...), custom_call_target="tpu_custom_call" | custom-call | tf_op jit(solution)/shard_map/pallas_call | solution.py:712
  1539.0 32.1 %shard_map.580 = (bf16[1,704,704]{2,1,0:T(8,128)(2,1)S(1)}, f32[2,4224]{1,0:T(2,128)S(1)}, f32[2,4224]{1,0:T(2,128)S(1)}, f32[2,4224]{1,0:T(2,128)S(1)}, f32[8,128]{1,0:T(8,128)S(1)}) custom-call(bf16[1,704,704]{2,1,0:T(8,128)(2,1)S(1)} %get-tuple-element.646.refs_0_, f32[2,4224]{1,0:T(2,128)S(1)} %select_add_fusion.1.refs_1_.refs_2_.refs_3_, ...), custom_call_target="tpu_custom_call" | custom-call | tf_op jit(solution)/shard_map/pallas_call | solution.py:712
  (1537 shorter events, 1165.9 us)
Async XLA Ops:
  7.2 132.2 %all-gather.15.cloned.1.call-start = ((), (), s32[]{:S(2)}) async-start(), calls=%async_computation.24 | async-start | bytes 4055040 | tf_op jit(solution)/shard_map/all_gather | solution.py:792
  32.8 113.9 %all-gather.17.cloned.1.call-start = ((), (), s32[]{:S(2)}) async-start(), calls=%async_computation.25 | async-start | bytes 1966080 | tf_op jit(solution)/shard_map/all_gather | solution.py:792
  45.4 236.7 %all-gather.21.cloned.1.call-start = ((), (), s32[]{:S(2)}) async-start(), calls=%async_computation.27 | async-start | bytes 2703360 | tf_op jit(solution)/shard_map/all_gather | solution.py:792
  56.7 227.5 %all-gather.19.cloned.1.call-start = ((), (), s32[]{:S(2)}) async-start(), calls=%async_computation.26 | async-start | bytes 5406720 | tf_op jit(solution)/shard_map/all_gather | solution.py:792
  91.4 306.3 %all-gather.23.cloned.1.call-start = ((), (), s32[]{:S(2)}) async-start(), calls=%async_computation.28 | async-start | bytes 2703360 | tf_op jit(solution)/shard_map/all_gather | solution.py:792
  148.0 417.6 %all-gather.25.cloned.1.call-start = ((), (), s32[]{:S(2)}) async-start(), calls=%async_computation.29 | async-start | bytes 2703360 | tf_op jit(solution)/shard_map/all_gather | solution.py:792
  148.3 109.8 %collective-permute-start.28 = (bf16[4,4,64,704]{3,2,1,0:T(8,128)(2,1)}, bf16[4,4,64,704]{3,2,1,0:T(8,128)(2,1)}, u32[]{:S(2)}, u32[]{:S(2)}) collective-permute-start(bf16[4,4,64,704]{3,2,1,0:T(8,128)(2,1)} %shard_map.474.refs_0_), channel_id=1, source_target_pairs={{0,1},{1,0},{2,3},{3,2},{4,5},{5,4},{6,7},{7,6},{8,9},{9,8},{10,11... | collective-permute-start | bytes 4325384 | tf_op jit(solution)/shard_map/ppermute | solution.py:489
  282.1 133.8 %collective-permute-start.33 = (bf16[4,1,88,3072]{3,2,1,0:T(8,128)(2,1)}, bf16[4,1,88,3072]{3,2,1,0:T(8,128)(2,1)}, u32[]{:S(2)}, u32[]{:S(2)}) collective-permute-start(bf16[4,1,88,3072]{3,2,1,0:T(8,128)(2,1)} %shard_map.489.refs_0_), channel_id=1, source_target_pairs={{0,4},{2,6},{4,0},{6,2},{1,5},{3,7},{5,1},{7,3},{8,12},{10,14},{12... | collective-permute-start | bytes 6488072 | tf_op jit(solution)/shard_map/ppermute | solution.py:485
  326.4 314.8 %all-gather.27.cloned.1.call-start = ((), (), s32[]{:S(2)}) async-start(), calls=%async_computation.30 | async-start | bytes 2703360 | tf_op jit(solution)/shard_map/all_gather | solution.py:792
  504.7 581.3 %reduce-scatter.15.cloned.1.call-start = ((), (), s32[]{:S(2)}) async-start(), calls=%async_computation.13 | async-start | bytes 2703360 | tf_op jit(solution)/shard_map/reduce_scatter | solution.py:959
  783.8 114.3 %collective-permute-start.60 = (bf16[1,352,3072]{2,1,0:T(8,128)(2,1)}, bf16[1,352,3072]{2,1,0:T(8,128)(2,1)}, u32[]{:S(2)}, u32[]{:S(2)}) collective-permute-start(bf16[1,352,3072]{2,1,0:T(8,128)(2,1)} %get-tuple-element.498), channel_id=1, source_target_pairs={{0,4},{2,6},{4,0},{6,2},{1,5},{3,7},{5,1},{7,3},{8,12},{10,14},{12... | collective-permute-start | bytes 6488072 | tf_op jit(solution)/shard_map/ppermute | solution.py:485
  799.3 105.4 %collective-permute-start.63 = (bf16[1,352,3072]{2,1,0:T(8,128)(2,1)}, bf16[1,352,3072]{2,1,0:T(8,128)(2,1)}, u32[]{:S(2)}, u32[]{:S(2)}) collective-permute-start(bf16[1,352,3072]{2,1,0:T(8,128)(2,1)} %get-tuple-element.506), channel_id=1, source_target_pairs={{0,4},{2,6},{4,0},{6,2},{1,5},{3,7},{5,1},{7,3},{8,12},{10,14},{12... | collective-permute-start | bytes 6488072 | tf_op jit(solution)/shard_map/ppermute | solution.py:485
  909.0 177.0 %reduce-scatter.13.cloned.1.call-start = ((), (), s32[]{:S(2)}) async-start(), calls=%async_computation.12 | async-start | bytes 2703360 | tf_op jit(solution)/shard_map/reduce_scatter | solution.py:959
  909.8 320.6 %reduce-scatter.17.cloned.1.call-start = ((), (), s32[]{:S(2)}) async-start(), calls=%async_computation.14 | async-start | bytes 1351680 | tf_op jit(solution)/shard_map/reduce_scatter | solution.py:959
  978.8 122.4 %collective-permute-start.72 = (bf16[4,352,704]{2,1,0:T(8,128)(2,1)}, bf16[4,352,704]{2,1,0:T(8,128)(2,1)}, u32[]{:S(2)}, u32[]{:S(2)}) collective-permute-start(bf16[4,352,704]{2,1,0:T(8,128)(2,1)} %get-tuple-element.541), channel_id=1, source_target_pairs={{0,4},{2,6},{4,0},{6,2},{1,5},{3,7},{5,1},{7,3},{8,12},{10,14},{12... | collective-permute-start | bytes 5947400 | tf_op jit(solution)/shard_map/ppermute | solution.py:485
  1038.7 191.7 %reduce-scatter.19.cloned.1.call-start = ((), (), s32[]{:S(2)}) async-start(), calls=%async_computation.15 | async-start | bytes 2703360 | tf_op jit(solution)/shard_map/reduce_scatter | solution.py:959
  1106.5 258.8 %reduce-scatter.21.cloned.1.call-start = ((), (), s32[]{:S(2)}) async-start(), calls=%async_computation.16 | async-start | bytes 983040 | tf_op jit(solution)/shard_map/reduce_scatter | solution.py:959
  1107.2 145.8 %collective-permute-start.81 = (bf16[1,352,3072]{2,1,0:T(8,128)(2,1)}, bf16[1,352,3072]{2,1,0:T(8,128)(2,1)}, u32[]{:S(2)}, u32[]{:S(2)}) collective-permute-start(bf16[1,352,3072]{2,1,0:T(8,128)(2,1)} %get-tuple-element.585), channel_id=1, source_target_pairs={{0,4},{2,6},{4,0},{6,2},{1,5},{3,7},{5,1},{7,3},{8,12},{10,14},{12... | collective-permute-start | bytes 6488072 | tf_op jit(solution)/shard_map/ppermute | solution.py:485
  1141.2 119.5 %collective-permute-start.85 = (bf16[1,352,3072]{2,1,0:T(8,128)(2,1)}, bf16[1,352,3072]{2,1,0:T(8,128)(2,1)}, u32[]{:S(2)}, u32[]{:S(2)}) collective-permute-start(bf16[1,352,3072]{2,1,0:T(8,128)(2,1)} %get-tuple-element.595), channel_id=1, source_target_pairs={{0,4},{2,6},{4,0},{6,2},{1,5},{3,7},{5,1},{7,3},{8,12},{10,14},{12... | collective-permute-start | bytes 6488072 | tf_op jit(solution)/shard_map/ppermute | solution.py:485
  1182.2 246.6 %reduce-scatter.23.cloned.1.call-start = ((), (), s32[]{:S(2)}) async-start(), calls=%async_computation.17 | async-start | bytes 2703360 | tf_op jit(solution)/shard_map/reduce_scatter | solution.py:959
  1264.5 179.6 %reduce-scatter.25.cloned.1.call-start = ((), (), s32[]{:S(2)}) async-start(), calls=%async_computation.18 | async-start | bytes 1351680 | tf_op jit(solution)/shard_map/reduce_scatter | solution.py:959
  1313.9 138.6 %reduce-scatter.35.cloned.1.call-start = ((), (), s32[]{:S(2)}) async-start(), calls=%async_computation.23 | async-start | bytes 2703360 | tf_op jit(solution)/shard_map/reduce_scatter | solution.py:959
  1316.3 210.7 %reduce-scatter.29.cloned.1.call-start = ((), (), s32[]{:S(2)}) async-start(), calls=%async_computation.20 | async-start | bytes 983040 | tf_op jit(solution)/shard_map/reduce_scatter | solution.py:959
  1459.3 174.4 %reduce-scatter.31.cloned.1.call-start = ((), (), s32[]{:S(2)}) async-start(), calls=%async_computation.21 | async-start | bytes 2703360 | tf_op jit(solution)/shard_map/reduce_scatter | solution.py:959
  (565 other events, 7976.8 us)
Sparse Core Ops, SparseCore 0:
  33.0 75.6 all-gather.14
  110.8 35.6 all-gather.16
  148.6 46.0 all-gather.20
  196.8 81.6 all-gather.18
  280.4 45.7 all-gather.22
  328.2 45.9 all-gather.24
  504.9 45.5 all-gather.26
  909.1 43.0 reduce-scatter.14
  955.2 44.2 reduce-scatter.12
  1038.8 25.7 reduce-scatter.16
  1106.6 43.1 reduce-scatter.18
  1182.3 21.7 reduce-scatter.20
  1264.6 48.2 reduce-scatter.22
  1315.6 27.0 reduce-scatter.24
  1345.4 43.5 reduce-scatter.34
  1448.9 24.6 reduce-scatter.28
  1476.4 26.9 reduce-scatter.26
  1576.8 43.2 reduce-scatter.30
  1636.6 26.8 reduce-scatter.32

commit v2 on v1

--- a/solution.py
+++ b/solution.py
@@ -1281,8 +1281,9 @@
     attended = (attn_own,) if last else (attn_own, swap_context(attn_given, CHIP))
     crossed = sum_parts(*crossed, order)
     crossed = (crossed[0], swap_context(crossed[1], CHIP))
-    texts = sum_parts(*texts, order)
-    texts = (texts[0], swap_context(texts[1], CHIP))
+    if last:
+        texts = sum_parts(*texts, order)
+        texts = (texts[0], swap_context(texts[1], CHIP))
     grad_shift_a = per_sequence(attn_in_grad, seqs)
     grad_scale_a = per_sequence(attn_in_grad * layer_norm(kept.after_skip), seqs)
     grad_res = grad_res + layer_norm_back(kept.after_skip, attn_in_grad * (1.0 + scale_a))
@@ -1306,12 +1307,14 @@
     def start():
         later.skipped = product([[kept.concat_low]], skip_grad, (0,) * parts, parts)
         reduced.cross = sum_rest(*crossed, order)
+        later.texts = sum_parts(*texts, order)
+        later.texts = (later.texts[0], swap_context(later.texts[1], CHIP))
 
     def first():
         reduced.attention = sum_rest(*attended, order)
 
     def second():
-        reduced.text = sum_rest(*texts, order)
+        reduced.text = sum_rest(*later.texts, order)
         kept, given = sum_parts(*later.skipped, order)
         later.skipped = (kept, swap_context(given, CHIP))
 

time: 1690 us -> 1660 us (0.982)
  waiting for transfers between devices: 431 us -> 401 us
    ppermute x41, waiting for transfers between devices: 173 us -> 141 us  [swap_tensor(): lax.ppermute(in_rows(operand), TENSOR, [(0, 1), (1, 0)])]
    unnamed x920 -> x914, local copies, waits for them, and re-layouts: 192 us -> 194 us
  transfers between devices with their start and end apart: 143 -> 143, of which waited for: 48 -> 46; matrix products, arithmetic and copies ran while one was open for 10% -> 10% of each run, Pallas kernels for 42% -> 42%
where the time goes in v2:
time: 1660 us; the launch traced here: 1650 us
  Pallas kernels  753 us (45%)
  waiting for transfers between devices  401 us (24%)
  local copies, waits for them, and re-layouts  219 us (13%)
  starting transfers between devices  132 us (8%)
  other arithmetic  113 us (7%)
  between operations  19.8 us (1%)
    ppermute x65, waiting for transfers between devices, swap_context(): return lax.ppermute(in_rows(operand), CONTEXT, pairs).reshape(operand.shape)  237 us
    unnamed x914, local copies, waits for them, and re-layouts  194 us
    pallas_call x12, Pallas kernels, grad_core(): pl.pallas_call(lambda *refs: grad_kernel(which, spread, tile, counts, len...  182 us
    pallas_call x32, Pallas kernels, multiply(): pl.pallas_call(kernel, grid=(pl.cdiv(width, tile),), in_specs=[pl.BlockSp...  170 us
    ppermute x41, waiting for transfers between devices, swap_tensor(): lax.ppermute(in_rows(operand), TENSOR, [(0, 1), (1, 0)])  141 us
    pallas_call x11, Pallas kernels, share_core(): pl.pallas_call(lambda *refs: share_kernel(count, places, *refs), in_specs...  106 us
    pallas_call x2, Pallas kernels, exchange(): pl.pallas_call(lambda *refs: exchange_kernel(list(kinds), *refs), in_spec...  89.3 us
    ppermute x65, starting transfers between devices, swap_context(): return lax.ppermute(in_rows(operand), CONTEXT, pairs).reshape(operand.shape)  49.3 us
  transfers between devices with their start and end apart: 143, of which 46 were waited for; matrix products, arithmetic and copies ran while one was open for 10% of the time, Pallas kernels for 42%

profile of v2, /device:TPU:0, one launch (start us, length us, event | category | flops | bytes accessed | tf_op | source)
XLA Modules:
  0.0 1645.5 jit_solution(3221822153119308727)
XLA Ops:
  72.7 15.0 collective-permute-done.3.refs_0_
  93.3 21.1 %collective-permute-done.5.refs_3_.refs_1_ = bf16[4,1,176,704]{3,2,1,0:T(8,128)(2,1)S(1)} collective-permute-done((bf16[4,1,176,704]{3,2,1,0:T(8,128)(2,1)}, bf16[4,1,176,704]{3,2,1,0:T(8,128)(2,1)S(1)}, u32[]{:S(2)}, u32[]{:S(2)}) %collective-permute-start.5) | collective-permute-done | bytes 991264 | tf_op jit(solution)/shard_map/ppermute | solution.py:489
  153.3 39.5 %collective-permute-done.16.refs_1_ = bf16[4,4,88,704]{3,2,1,0:T(8,128)(2,1)} collective-permute-done((bf16[4,4,88,704]{3,2,1,0:T(8,128)(2,1)}, bf16[4,4,88,704]{3,2,1,0:T(8,128)(2,1)}, u32[]{:S(2)}, u32[]{:S(2)}) %collective-permute-start.16) | collective-permute-done | bytes 1982496 | tf_op jit(solution)/shard_map/ppermute | solution.py:485
  226.5 16.8 %collective-permute-done.17 = bf16[64,8,704]{2,1,0:T(8,128)(2,1)} collective-permute-done((bf16[64,8,704]{2,1,0:T(8,128)(2,1)}, bf16[64,8,704]{2,1,0:T(8,128)(2,1)}, u32[]{:S(2)}, u32[]{:S(2)}) %collective-permute-start.17) | collective-permute-done | bytes 720928 | tf_op jit(solution)/shard_map/ppermute | solution.py:485
  243.4 14.7 collective-permute-done.20
  334.0 15.4 shard_map.477
  358.8 17.0 %collective-permute-done.30.refs_0_ = bf16[4,2,88,704]{3,2,1,0:T(8,128)(2,1)} collective-permute-done((bf16[4,2,88,704]{3,2,1,0:T(8,128)(2,1)}, bf16[4,2,88,704]{3,2,1,0:T(8,128)(2,1)}, u32[]{:S(2)}, u32[]{:S(2)}) %collective-permute-start.30) | collective-permute-done | bytes 991264 | tf_op jit(solution)/shard_map/ppermute | solution.py:485
  433.0 17.0 %collective-permute-done.32.refs_1_ = bf16[256,1408]{1,0:T(8,128)(2,1)S(1)} collective-permute-done((bf16[256,1408]{1,0:T(8,128)(2,1)S(1)}, bf16[256,1408]{1,0:T(8,128)(2,1)S(1)}, u32[]{:S(2)}, u32[]{:S(2)}) %collective-permute-start.32) | collective-permute-done | bytes 720928 | tf_op jit(solution)/shard_map/ppermute | solution.py:489
  475.6 17.9 %collective-permute-done.35.refs_3_.refs_1_ = bf16[4,4,88,704]{3,2,1,0:T(8,128)(2,1)} collective-permute-done((bf16[4,4,88,704]{3,2,1,0:T(8,128)(2,1)}, bf16[4,4,88,704]{3,2,1,0:T(8,128)(2,1)}, u32[]{:S(2)}, u32[]{:S(2)}) %collective-permute-start.35) | collective-permute-done | bytes 1982496 | tf_op jit(solution)/shard_map/ppermute | solution.py:485
  584.4 16.8 %collective-permute-done.42 = bf16[64,8,704]{2,1,0:T(8,128)(2,1)} collective-permute-done((bf16[64,8,704]{2,1,0:T(8,128)(2,1)}, bf16[64,8,704]{2,1,0:T(8,128)(2,1)}, u32[]{:S(2)}, u32[]{:S(2)}) %collective-permute-start.42) | collective-permute-done | bytes 720928 | tf_op jit(solution)/shard_map/ppermute | solution.py:485
  691.0 16.3 collective-permute-done.50.refs_1_
  784.5 14.7 shard_map.525
  855.6 14.8 shard_map.531
  874.9 21.9 %shard_map.533 = (bf16[2,2,128,704]{3,2,1,0:T(8,128)(2,1)}, bf16[2,2,128,704]{3,2,1,0:T(8,128)(2,1)}, bf16[2,2,128,704]{3,2,1,0:T(8,128)(2,1)}, bf16[2,2,128,704...) custom-call(bf16[2,2,128,704]{3,2,1,0:T(8,128)(2,1)} %bitcast.716, ...), custom_call_target="tpu_custom_call" | custom-call | flops 10737418 | bytes 14417 | tf_op jit(solution)/shard_map/pallas_call | solution.py:283
  931.0 15.7 collective-permute-done.62
  1057.0 15.1 shard_map.549
  1097.2 14.9 shard_map.551
  1161.1 16.1 shard_map.558
  1177.2 20.6 %shard_map.559 = (bf16[2,256,704]{2,1,0:T(8,128)(2,1)}, bf16[2,256,704]{2,1,0:T(8,128)(2,1)}, bf16[2,256,704]{2,1,0:T(8,128)(2,1)}, bf16[2,256,704]{2,1,0:T(8,128)(2,1)}, f32[8,128]{1,0:T(8,128)}) custom-call(bf16[768,1024]{1,0:T(8,128)(2,1)} %bitcast.599, bf16[768,704]{1,0:T(8,128)(2,1)} %bitcast.684, bf16[768,704]{1,0:T(8,128)(2,1)} %bitcast.688, ...), custom_call_target="tpu_custom_call" | custom-call | flops 4429185 | bytes 4325 | tf_op jit(solution)/shard_map/pallas_call | solution.py:924
  1202.5 21.9 %shard_map.561 = (bf16[2,2,128,704]{3,2,1,0:T(8,128)(2,1)}, bf16[2,2,128,704]{3,2,1,0:T(8,128)(2,1)}, bf16[2,2,128,704]{3,2,1,0:T(8,128)(2,1)}, bf16[2,2,128,704...) custom-call(bf16[2,2,128,704]{3,2,1,0:T(8,128)(2,1)} %bitcast.731, ...), custom_call_target="tpu_custom_call" | custom-call | flops 10737418 | bytes 14417 | tf_op jit(solution)/shard_map/pallas_call | solution.py:283
  1337.4 16.6 %shard_map.570 = (bf16[4,352,704]{2,1,0:T(8,128)(2,1)}, bf16[4,352,704]{2,1,0:T(8,128)(2,1)}, f32[8,128]{1,0:T(8,128)}) custom-call(bf16[256,1408]{1,0:T(8,128)(2,1)} %copy-done.109, bf16[256,1408]{1,0:T(8,128)(2,1)} %copy-done.232, bf16[256,1408]{1,0:T(8,128)(2,1)} %copy-done.107, bf16[256,1408]{1,0:T(8,128)(2,1)} %copy-done.230, ...), custom_call_target="tpu_custom_call" | custom-call | flops 4060086 | bytes 5947 | tf_op jit(solution)/shard_map/pallas_call | solution.py:924
  1400.9 15.2 shard_map.574
  1433.9 57.2 %shard_map.577 = (bf16[1,704,704]{2,1,0:T(8,128)(2,1)S(1)}, bf16[1,704,704]{2,1,0:T(8,128)(2,1)S(1)}, bf16[4,352,704]{2,1,0:T(8,128)(2,1)S(1)}, f32[2,4224]{1,0:T(2,128)S(1)}, f32[8,128]{1,0:T(8,128)S(1)}) custom-call(bf16[1,704,704]{2,1,0:T(8,128)(2,1)S(1)} %copy-done.272, bf16[1,704,704]{2,1,0:T(8,128)(2,1)S(1)} %copy-done.273, ...), custom_call_target="tpu_custom_call" | custom-call | tf_op jit(solution)/shard_map/pallas_call | solution.py:712
  1511.1 32.1 %shard_map.580 = (bf16[1,704,704]{2,1,0:T(8,128)(2,1)S(1)}, f32[2,4224]{1,0:T(2,128)S(1)}, f32[2,4224]{1,0:T(2,128)S(1)}, f32[2,4224]{1,0:T(2,128)S(1)}, f32[8,128]{1,0:T(8,128)S(1)}) custom-call(bf16[1,704,704]{2,1,0:T(8,128)(2,1)S(1)} %get-tuple-element.646.refs_0_, f32[2,4224]{1,0:T(2,128)S(1)} %select_add_fusion.1.refs_1_.refs_2_.refs_3_, ...), custom_call_target="tpu_custom_call" | custom-call | tf_op jit(solution)/shard_map/pallas_call | solution.py:712
  (1531 shorter events, 1141.3 us)
Async XLA Ops:
  7.2 132.2 %all-gather.15.cloned.1.call-start = ((), (), s32[]{:S(2)}) async-start(), calls=%async_computation.24 | async-start | bytes 4055040 | tf_op jit(solution)/shard_map/all_gather | solution.py:792
  32.8 113.9 %all-gather.17.cloned.1.call-start = ((), (), s32[]{:S(2)}) async-start(), calls=%async_computation.25 | async-start | bytes 1966080 | tf_op jit(solution)/shard_map/all_gather | solution.py:792
  45.4 236.7 %all-gather.21.cloned.1.call-start = ((), (), s32[]{:S(2)}) async-start(), calls=%async_computation.27 | async-start | bytes 2703360 | tf_op jit(solution)/shard_map/all_gather | solution.py:792
  56.7 227.5 %all-gather.19.cloned.1.call-start = ((), (), s32[]{:S(2)}) async-start(), calls=%async_computation.26 | async-start | bytes 5406720 | tf_op jit(solution)/shard_map/all_gather | solution.py:792
  91.4 306.3 %all-gather.23.cloned.1.call-start = ((), (), s32[]{:S(2)}) async-start(), calls=%async_computation.28 | async-start | bytes 2703360 | tf_op jit(solution)/shard_map/all_gather | solution.py:792
  148.0 417.7 %all-gather.25.cloned.1.call-start = ((), (), s32[]{:S(2)}) async-start(), calls=%async_computation.29 | async-start | bytes 2703360 | tf_op jit(solution)/shard_map/all_gather | solution.py:792
  148.3 109.8 %collective-permute-start.28 = (bf16[4,4,64,704]{3,2,1,0:T(8,128)(2,1)}, bf16[4,4,64,704]{3,2,1,0:T(8,128)(2,1)}, u32[]{:S(2)}, u32[]{:S(2)}) collective-permute-start(bf16[4,4,64,704]{3,2,1,0:T(8,128)(2,1)} %shard_map.474.refs_0_), channel_id=1, source_target_pairs={{0,1},{1,0},{2,3},{3,2},{4,5},{5,4},{6,7},{7,6},{8,9},{9,8},{10,11... | collective-permute-start | bytes 4325384 | tf_op jit(solution)/shard_map/ppermute | solution.py:489
  282.1 133.8 %collective-permute-start.33 = (bf16[4,1,88,3072]{3,2,1,0:T(8,128)(2,1)}, bf16[4,1,88,3072]{3,2,1,0:T(8,128)(2,1)}, u32[]{:S(2)}, u32[]{:S(2)}) collective-permute-start(bf16[4,1,88,3072]{3,2,1,0:T(8,128)(2,1)} %shard_map.489.refs_0_), channel_id=1, source_target_pairs={{0,4},{2,6},{4,0},{6,2},{1,5},{3,7},{5,1},{7,3},{8,12},{10,14},{12... | collective-permute-start | bytes 6488072 | tf_op jit(solution)/shard_map/ppermute | solution.py:485
  326.3 314.9 %all-gather.27.cloned.1.call-start = ((), (), s32[]{:S(2)}) async-start(), calls=%async_computation.30 | async-start | bytes 2703360 | tf_op jit(solution)/shard_map/all_gather | solution.py:792
  504.8 552.2 %reduce-scatter.15.cloned.1.call-start = ((), (), s32[]{:S(2)}) async-start(), calls=%async_computation.13 | async-start | bytes 2703360 | tf_op jit(solution)/shard_map/reduce_scatter | solution.py:959
  783.7 114.2 %collective-permute-start.60 = (bf16[1,352,3072]{2,1,0:T(8,128)(2,1)}, bf16[1,352,3072]{2,1,0:T(8,128)(2,1)}, u32[]{:S(2)}, u32[]{:S(2)}) collective-permute-start(bf16[1,352,3072]{2,1,0:T(8,128)(2,1)} %get-tuple-element.498), channel_id=1, source_target_pairs={{0,4},{2,6},{4,0},{6,2},{1,5},{3,7},{5,1},{7,3},{8,12},{10,14},{12... | collective-permute-start | bytes 6488072 | tf_op jit(solution)/shard_map/ppermute | solution.py:485
  799.3 105.3 %collective-permute-start.63 = (bf16[1,352,3072]{2,1,0:T(8,128)(2,1)}, bf16[1,352,3072]{2,1,0:T(8,128)(2,1)}, u32[]{:S(2)}, u32[]{:S(2)}) collective-permute-start(bf16[1,352,3072]{2,1,0:T(8,128)(2,1)} %get-tuple-element.506), channel_id=1, source_target_pairs={{0,4},{2,6},{4,0},{6,2},{1,5},{3,7},{5,1},{7,3},{8,12},{10,14},{12... | collective-permute-start | bytes 6488072 | tf_op jit(solution)/shard_map/ppermute | solution.py:485
  909.0 148.0 %reduce-scatter.13.cloned.1.call-start = ((), (), s32[]{:S(2)}) async-start(), calls=%async_computation.12 | async-start | bytes 2703360 | tf_op jit(solution)/shard_map/reduce_scatter | solution.py:959
  909.7 292.8 %reduce-scatter.17.cloned.1.call-start = ((), (), s32[]{:S(2)}) async-start(), calls=%async_computation.14 | async-start | bytes 1351680 | tf_op jit(solution)/shard_map/reduce_scatter | solution.py:959
  980.9 91.3 %collective-permute-start.72 = (bf16[4,352,704]{2,1,0:T(8,128)(2,1)}, bf16[4,352,704]{2,1,0:T(8,128)(2,1)}, u32[]{:S(2)}, u32[]{:S(2)}) collective-permute-start(bf16[4,352,704]{2,1,0:T(8,128)(2,1)} %get-tuple-element.541), channel_id=1, source_target_pairs={{0,4},{2,6},{4,0},{6,2},{1,5},{3,7},{5,1},{7,3},{8,12},{10,14},{12... | collective-permute-start | bytes 5947400 | tf_op jit(solution)/shard_map/ppermute | solution.py:485
  1009.8 192.7 %reduce-scatter.19.cloned.1.call-start = ((), (), s32[]{:S(2)}) async-start(), calls=%async_computation.15 | async-start | bytes 2703360 | tf_op jit(solution)/shard_map/reduce_scatter | solution.py:959
  1077.4 259.9 %reduce-scatter.21.cloned.1.call-start = ((), (), s32[]{:S(2)}) async-start(), calls=%async_computation.16 | async-start | bytes 983040 | tf_op jit(solution)/shard_map/reduce_scatter | solution.py:959
  1078.9 146.2 %collective-permute-start.81 = (bf16[1,352,3072]{2,1,0:T(8,128)(2,1)}, bf16[1,352,3072]{2,1,0:T(8,128)(2,1)}, u32[]{:S(2)}, u32[]{:S(2)}) collective-permute-start(bf16[1,352,3072]{2,1,0:T(8,128)(2,1)} %get-tuple-element.585), channel_id=1, source_target_pairs={{0,4},{2,6},{4,0},{6,2},{1,5},{3,7},{5,1},{7,3},{8,12},{10,14},{12... | collective-permute-start | bytes 6488072 | tf_op jit(solution)/shard_map/ppermute | solution.py:485
  1112.1 120.7 %collective-permute-start.85 = (bf16[1,352,3072]{2,1,0:T(8,128)(2,1)}, bf16[1,352,3072]{2,1,0:T(8,128)(2,1)}, u32[]{:S(2)}, u32[]{:S(2)}) collective-permute-start(bf16[1,352,3072]{2,1,0:T(8,128)(2,1)} %get-tuple-element.595), channel_id=1, source_target_pairs={{0,4},{2,6},{4,0},{6,2},{1,5},{3,7},{5,1},{7,3},{8,12},{10,14},{12... | collective-permute-start | bytes 6488072 | tf_op jit(solution)/shard_map/ppermute | solution.py:485
  1153.9 246.9 %reduce-scatter.23.cloned.1.call-start = ((), (), s32[]{:S(2)}) async-start(), calls=%async_computation.17 | async-start | bytes 2703360 | tf_op jit(solution)/shard_map/reduce_scatter | solution.py:959
  1236.5 179.6 %reduce-scatter.25.cloned.1.call-start = ((), (), s32[]{:S(2)}) async-start(), calls=%async_computation.18 | async-start | bytes 1351680 | tf_op jit(solution)/shard_map/reduce_scatter | solution.py:959
  1286.0 138.6 %reduce-scatter.35.cloned.1.call-start = ((), (), s32[]{:S(2)}) async-start(), calls=%async_computation.23 | async-start | bytes 2703360 | tf_op jit(solution)/shard_map/reduce_scatter | solution.py:959
  1288.4 210.7 %reduce-scatter.29.cloned.1.call-start = ((), (), s32[]{:S(2)}) async-start(), calls=%async_computation.20 | async-start | bytes 983040 | tf_op jit(solution)/shard_map/reduce_scatter | solution.py:959
  1431.4 174.4 %reduce-scatter.31.cloned.1.call-start = ((), (), s32[]{:S(2)}) async-start(), calls=%async_computation.21 | async-start | bytes 2703360 | tf_op jit(solution)/shard_map/reduce_scatter | solution.py:959
  (562 other events, 7721.0 us)
Sparse Core Ops, SparseCore 0:
  33.0 75.6 all-gather.14
  110.8 35.6 all-gather.16
  148.6 46.0 all-gather.20
  196.8 81.6 all-gather.18
  280.4 45.7 all-gather.22
  328.2 45.9 all-gather.24
  504.9 45.5 all-gather.26
  909.1 43.0 reduce-scatter.14
  955.2 44.2 reduce-scatter.12
  1009.9 26.1 reduce-scatter.16
  1077.6 43.6 reduce-scatter.18
  1154.1 22.0 reduce-scatter.20
  1236.7 48.2 reduce-scatter.22
  1287.7 27.0 reduce-scatter.24
  1317.5 43.5 reduce-scatter.34
  1421.0 24.6 reduce-scatter.28
  1448.5 26.9 reduce-scatter.26
  1548.9 43.2 reduce-scatter.30
  1608.7 26.8 reduce-scatter.32
